TPU v7x, 256 devices: a whole 4x4x8 slice. The times are simulated.
256 devices in a mesh: pipe: 32 (over x, z_hi, y), tensor: 4 (over z_lo), dp: 2 (over core).
Axes of the slice: x: 4, y: 4, z: 8 (z_hi: 2, z_lo: 4; z = z_hi * 4 + z_lo), core: 2. Of those that a mesh axis runs over, the one named last changes fastest.
Arguments:
- hidden: bfloat16 [512, 5120], P('dp', ('pipe', 'tensor')), may hold values from -16 to 16
- head_weight: bfloat16 [151936, 5120], P(('pipe', 'tensor'), 'dp'), may hold values from -2 to 2
- labels: int32 [512], P('dp'), may hold values from 0 to 151935
- loss_weight: float32 [512], P('dp'), may hold values from 1 to 10
Outputs:
- hidden_grad: bfloat16 [512, 5120], P('dp', ('pipe', 'tensor'))
- head_grad: bfloat16 [151936, 5120], P(('pipe', 'tensor'), 'dp')
- token_loss: float32 [512], P('dp')
All inputs are finite; a program needn't handle non-finite values.
Results may differ from a plain program's by a relative error of at most 0.0052.
Values may be sent and summed in bfloat16 or wider, within the bound.
No kernel may reach another device: no remote copies, remote signals or barrier semaphores. Data moves between devices by JAX's collectives and lax.ppermute only.
A program may use at most 128 MiB of HBM per device.

v0:
```python
import jax
import jax.numpy as jnp
from jax import lax
from jax.sharding import PartitionSpec as P


def per_device(hidden, head_weight, labels, loss_weight):
    features = lax.all_gather(hidden, ("pipe", "tensor"), axis=1, tiled=True)
    full_weight = lax.all_gather(head_weight, "dp", axis=1, tiled=True)
    logits = lax.dot_general(
        full_weight, features, (((1,), (1,)), ((), ())), preferred_element_type=jnp.float32
    )
    slice_rows = full_weight.shape[0]
    first_entry = lax.axis_index(("pipe", "tensor")) * slice_rows
    vocab_rows = first_entry + jnp.arange(slice_rows, dtype=jnp.int32)
    target_mask = (vocab_rows[:, None] == labels[None, :]).astype(jnp.float32)
    local_picked = jnp.sum(target_mask * logits, axis=0)
    row_peak = lax.pmax(jnp.max(logits, axis=0), ("pipe", "tensor"))
    shifted_exp = jnp.exp(logits - row_peak[None, :])
    row_total, picked = lax.psum((jnp.sum(shifted_exp, axis=0), local_picked), ("pipe", "tensor"))
    token_loss = row_peak + jnp.log(row_total) - picked
    logit_grad = (loss_weight[None, :] * (shifted_exp / row_total[None, :] - target_mask)).astype(
        jnp.bfloat16
    )
    grad_rows = lax.psum_scatter(
        lax.dot_general(
            full_weight, logit_grad, (((0,), (0,)), ((), ())), preferred_element_type=jnp.float32
        ),
        ("pipe", "tensor"),
        scatter_dimension=0,
        tiled=True,
    )
    hidden_grad = grad_rows.T.astype(jnp.bfloat16)
    weight_term = jnp.dot(logit_grad, features, preferred_element_type=jnp.float32)
    head_grad = lax.psum_scatter(weight_term, "dp", scatter_dimension=1, tiled=True).astype(
        jnp.bfloat16
    )
    return (hidden_grad, head_grad, token_loss)


def solution(mesh):
    return jax.shard_map(
        per_device,
        mesh=mesh,
        in_specs=(P("dp", ("pipe", "tensor")), P(("pipe", "tensor"), "dp"), P("dp"), P("dp")),
        out_specs=(P("dp", ("pipe", "tensor")), P(("pipe", "tensor"), "dp"), P("dp")),
        check_vma=False,
    )
```

profile of v0, /device:TPU:8, one launch (start us, length us, event | category | flops | bytes accessed | tf_op | source)
XLA Modules:
  0.0 2162.2 jit_solution(11261897426702758272)
XLA Ops:
  7.2 0.0 all-gather.5.cloned.1.call-start
  7.2 0.7 all-gather.5.cloned.1.call-update
  7.9 0.0 all-gather.3.cloned.1.call-start
  7.9 0.7 all-gather.3.cloned.1.call-update
  8.6 0.0 reduce-scatter.7.cloned.1.call-start
  8.7 0.0 copy-start
  8.7 652.2 %all-gather.5.cloned.1.call-done = bf16[256,5120]{0,1:T(8,128)(2,1)} async-done(((bf16[256,40]{0,1:T(8,128)(2,1)}), bf16[256,5120]{0,1:T(8,128)(2,1)}) %all-gather.5.cloned.1.call-update) | async-done | bytes 2621456 | tf_op jit(solution)/shard_map/all_gather | solution.py:8
  660.9 33.9 %all-gather.3.cloned.1.call-done = bf16[1187,5120]{1,0:T(8,128)(2,1)} async-done(((bf16[1187,2560]{1,0:T(8,128)(2,1)}), bf16[1187,5120]{1,0:T(8,128)(2,1)}) %all-gather.3.cloned.1.call-update) | async-done | bytes 12154896 | tf_op jit(solution)/shard_map/all_gather | solution.py:9
  694.8 7.2 fusion.7
  702.0 0.0 copy-start.1
  702.0 339.8 %pmax.7 = f32[256]{0:T(256)S(1)} all-reduce(f32[256]{0:T(256)S(1)} %get-tuple-element.13), channel_id=1, replica_groups=mesh['pipe'=32,'tensor'=4,'dp'=2] {'pipe','tensor'}, use_global_device_ids=true, to_apply=%region_1.0 | all-reduce | flops 256 | bytes 2048 | tf_op jit(solution)/shard_map/pmax | solution.py:18
  1041.8 0.0 copy-done
  1041.8 0.3 fusion.3
  1042.1 342.1 %all-reduce = (f32[256]{0:T(256)S(1)}, f32[256]{0:T(256)S(1)}) all-reduce(f32[256]{0:T(256)S(1)} %get-tuple-element.10, f32[256]{0:T(256)S(1)} %get-tuple-element.9), channel_id=1, replica_groups=mesh['pipe'=32,'tensor'=4,'dp'=2] {'pipe','tensor'}, use_global_device_ids=true, to_apply=%region_3.0 | all-reduce | flops 512 | bytes 4096 | tf_op jit(solution)/shard_map/psum | solution.py:20
  1384.3 0.0 copy-done.1
  1384.3 10.7 convolution_bitcast_fusion.1
  1395.0 5.9 copy.9
  1400.9 0.0 reduce-scatter.7.cloned.1.call-update
  1400.9 0.0 reduce-scatter.9.cloned.1.call-start
  1400.9 12.9 convolution_bitcast_fusion
  1413.8 0.0 reduce-scatter.9.cloned.1.call-update
  1413.8 0.6 add_subtract_fusion
  1414.4 683.6 %reduce-scatter.7.cloned.1.call-done = f32[40,256]{1,0:T(8,128)} async-done(((f32[5120,256]{1,0:T(8,128)}), f32[40,256]{1,0:T(8,128)}) %reduce-scatter.7.cloned.1.call-update) | async-done | bytes 40976
  2098.0 0.9 copy.10
  2098.9 0.7 copy.8
  2099.6 45.1 %reduce-scatter.9.cloned.1.call-done = f32[2560,1187]{1,0:T(8,128)} async-done(((f32[5120,1187]{1,0:T(8,128)}), f32[2560,1187]{1,0:T(8,128)}) %reduce-scatter.9.cloned.1.call-update) | async-done | bytes 12154896
  2144.6 11.0 copy.12
  (1 shorter events, 0.0 us)
Async XLA Ops:
  7.2 653.7 %all-gather.5.cloned.1.call-start = ((), (), s32[]{:S(2)}) async-start(), calls=%async_computation.3 | async-start | bytes 2641920 | tf_op jit(solution)/shard_map/all_gather | solution.py:8
  7.9 686.9 %all-gather.3.cloned.1.call-start = ((), (), s32[]{:S(2)}) async-start(), calls=%async_computation.2 | async-start | bytes 18309120 | tf_op jit(solution)/shard_map/all_gather | solution.py:9
  8.6 2089.3 %reduce-scatter.7.cloned.1.call-start = ((), (), s32[]{:S(2)}) async-start(), calls=%async_computation.4 | async-start | bytes 5283840
  8.7 1033.1 %copy-start = (s32[256]{0:T(256)S(1)}, s32[256]{0:T(256)}, u32[]{:S(2)}) copy-start(s32[256]{0:T(256)} %param.6) | copy-start | bytes 3076
  702.0 682.3 %copy-start.1 = (f32[256]{0:T(256)S(1)}, f32[256]{0:T(256)}, u32[]{:S(2)}) copy-start(f32[256]{0:T(256)} %param.7) | copy-start | bytes 3076
  1400.9 743.8 %reduce-scatter.9.cloned.1.call-start = ((), (), s32[]{:S(2)}) async-start(), calls=%async_computation.5 | async-start | bytes 39321600
Sparse Core Ops, SparseCore 0:
  9.8 651.0 all-gather.4
  662.7 32.0 all-gather.2
  1401.0 696.8 reduce-scatter.6
  2100.5 44.0 reduce-scatter.8
where the time goes:
time: 2160 us
  waiting for transfers between devices  1420 us (66%)
  blocking collectives  682 us (32%)
  matrix products  30.8 us (1%)
    unnamed x6, waiting for transfers between devices  730 us
    all_gather x1, waiting for transfers between devices, per_device(): features = lax.all_gather(hidden, ('pipe', 'tensor'), axis=1, tiled=True)  652 us
    psum x1, blocking collectives, per_device(): lax.psum((jnp.sum(shifted_exp, axis=0), local_picked), ('pipe', 'tensor'))  342 us
    pmax x1, blocking collectives, per_device(): row_peak = lax.pmax(jnp.max(logits, axis=0), ('pipe', 'tensor'))  340 us
  transfers between devices with their start and end apart: 4, of which 4 were waited for; matrix products, arithmetic and copies ran while one was open for 1% of the time, Pallas kernels for 0%

commit v1 on v0

v1 whole, which is shorter than its diff:
```python
import jax
import jax.numpy as jnp
from jax import lax
from jax.experimental import pallas as pl
from jax.experimental.pallas import tpu as pltpu
from jax.sharding import Mesh, PartitionSpec as P

BF = jnp.bfloat16
F32 = jnp.float32
HBM = pl.BlockSpec(memory_space=pltpu.HBM)
VMEM = pl.BlockSpec(memory_space=pltpu.VMEM)
SMEM = pl.BlockSpec(memory_space=pltpu.SMEM)
SECTIONS = ("x", "zh", "y", "t")


def paired(n, k):
    return [(i, i ^ k) for i in range(n)]


def spread(block, axis):
    got = {k: lax.ppermute(block, axis, paired(4, k)) for k in (2, 1, 3)}
    got[0] = block
    return [got[k] for k in range(4)]


def collect(blocks, axis):
    got = [lax.ppermute(blocks[k], axis, paired(4, k)) for k in (2, 1, 3)]
    total = blocks[0].astype(F32)
    for piece in got:
        total = total + piece.astype(F32)
    return total


def share(block, axes):
    n = lax.axis_size(axes)
    return lax.all_to_all(jnp.broadcast_to(block[None], (n,) + block.shape), axes, 0, 0)


def combine(every):
    peak = jnp.max(every[:, 0], axis=0)
    total = jnp.sum(every[:, 1] * jnp.exp(every[:, 0] - peak[None]), axis=0)
    return jnp.stack([peak, total, jnp.sum(every[:, 2], axis=0)])


def each_piece(pos, side, firsts, seconds, own, other, act):
    core, x, y = pos[0], pos[1], pos[2]
    for kx in range(4):
        place = x ^ kx ^ (2 * core)

        def visit(half):
            for zh in range(2):
                for ky in range(4):
                    block = ((place % 2) * 2 + zh) * 4 + (y ^ ky)
                    row = pl.multiple_of(block * 2 * side, 16)
                    act(firsts[ky], (kx, zh), half, pl.ds(row, side))
                    row = pl.multiple_of(block * 2 * side + side, 16)
                    act(seconds[kx], (ky, zh), half, pl.ds(row, side))

        pl.when(place < 2)(lambda: visit(own))
        pl.when(place >= 2)(lambda: visit(other))


def fetch(own_far, other_far, own, other, sems):
    copies = [
        pltpu.make_async_copy(own_far, own, sems.at[0]),
        pltpu.make_async_copy(other_far, other, sems.at[1]),
    ]
    for copy in copies:
        copy.start()
    return copies


def logits_kernel(pos, own_far, other_far, labels, a0, a1, a2, a3, b0, b1, b2, b3,
                  logits, stats, feats_own, feats_other, own, other, sems):
    copies = fetch(own_far, other_far, own, other, sems)

    def place(piece, index, half, rows):
        half[rows, :] = piece[index]

    firsts, seconds = (a0, a1, a2, a3), (b0, b1, b2, b3)
    each_piece(pos, a0.shape[2], firsts, seconds, feats_own, feats_other, place)
    copies[0].wait()
    logits[...] = jnp.dot(own[...], feats_own[...], preferred_element_type=F32)
    copies[1].wait()
    logits[...] += jnp.dot(other[...], feats_other[...], preferred_element_type=F32)
    value = logits[...]
    rows = lax.broadcasted_iota(jnp.int32, value.shape, 0) + pos[3]
    peak = jnp.max(value, axis=0, keepdims=True)
    stats[0:1, :] = peak
    stats[1:2, :] = jnp.sum(jnp.exp(value - peak), axis=0, keepdims=True)
    stats[2:3, :] = jnp.sum(jnp.where(rows == labels[...], value, 0.0), axis=0, keepdims=True)


def grad_kernel(pos, own_far, other_far, logits, labels, loss_weight, stats,
                grad, a0, a1, a2, a3, b0, b1, b2, b3,
                grad_t, part_own, part_other, own, other, sems):
    copies = fetch(own_far, other_far, own, other, sems)
    value = logits[...]
    rows = lax.broadcasted_iota(jnp.int32, value.shape, 0) + pos[3]
    target = jnp.where(rows == labels[...], 1.0, 0.0)
    result = loss_weight[...] * (jnp.exp(value - stats[0:1, :]) / stats[1:2, :] - target)
    grad[...] = result.astype(BF)
    grad_t[...] = result.T.astype(BF)
    width = own.shape[1] // 2
    for j in range(4):
        if j % 2 == 0:
            copies[j // 2].wait()
        weight, part = (own, part_own) if j < 2 else (other, part_other)
        span = slice((j % 2) * width, (j % 2 + 1) * width)
        piece = jnp.dot(grad_t[...], weight[:, span], preferred_element_type=F32)
        part[span, :] = piece.T.astype(BF)

    def take(piece, index, half, rows):
        piece[index] = half[rows, :]

    firsts, seconds = (a0, a1, a2, a3), (b0, b1, b2, b3)
    each_piece(pos, a0.shape[2], firsts, seconds, part_own, part_other, take)


def per_device(hidden, head_weight, labels, loss_weight):
    rows, half = head_weight.shape
    tokens, cols = hidden.shape
    side = 2 * cols
    swap = [(0, 1), (1, 0)]
    weight_other = lax.ppermute(head_weight, "dp", swap)
    pos = jnp.stack(
        [lax.axis_index("dp"), lax.axis_index("x"), lax.axis_index("y"),
         lax.axis_index(SECTIONS) * rows]
    ).astype(jnp.int32)
    labels = labels[None, :]
    loss_weight = loss_weight[None, :]
    params = pltpu.CompilerParams(vmem_limit_bytes=50 * 1024 * 1024)
    weights = [pltpu.VMEM((rows, half), BF)] * 2 + [pltpu.SemaphoreType.DMA((2,))]

    line = share(hidden.T, ("zh", "t")).reshape(2, 2, side, tokens)
    first = jnp.stack(spread(line[:, 0], "x"))
    second = jnp.stack(spread(line[:, 1], "y"))
    first, second, weight_other = lax.optimization_barrier((first, second, weight_other))
    first = spread(first, "y")
    second = spread(second, "x")
    logits, stats, feats_own, feats_other = pl.pallas_call(
        logits_kernel,
        in_specs=[SMEM] + [HBM] * 2 + [VMEM] * 9,
        out_specs=[VMEM] * 4,
        out_shape=[
            jax.ShapeDtypeStruct((rows, tokens), F32),
            jax.ShapeDtypeStruct((3, tokens), F32),
            jax.ShapeDtypeStruct((half, tokens), BF),
            jax.ShapeDtypeStruct((half, tokens), BF),
        ],
        scratch_shapes=weights,
        compiler_params=params,
        name="logits",
    )(pos, head_weight, weight_other, labels, *first, *second)

    stats = combine(share(stats, ("x", "y", "t")))
    stats, feats_other = lax.optimization_barrier((stats, feats_other))
    feats_peer = lax.ppermute(feats_other, "dp", swap)
    stats = combine(jnp.stack([stats, lax.ppermute(stats, "zh", swap)]))
    token_loss = stats[0] + jnp.log(stats[1]) - stats[2]

    outs = pl.pallas_call(
        grad_kernel,
        in_specs=[SMEM] + [HBM] * 2 + [VMEM] * 4,
        out_specs=[VMEM] * 9,
        out_shape=[jax.ShapeDtypeStruct((rows, tokens), BF)]
        + [jax.ShapeDtypeStruct(first[0].shape, BF)] * 8,
        scratch_shapes=[
            pltpu.VMEM((tokens, rows), BF),
            pltpu.VMEM((half, tokens), BF),
            pltpu.VMEM((half, tokens), BF),
        ] + weights,
        compiler_params=params,
        name="grads",
    )(pos, head_weight, weight_other, logits, labels, loss_weight, stats)
    grad = outs[0]

    first = collect(outs[1:5], "y").astype(BF)
    second = collect(outs[5:9], "x").astype(BF)
    first, second, grad = lax.optimization_barrier((first, second, grad))
    grad_peer = lax.ppermute(grad, "dp", swap)
    dot = lambda a, b: lax.dot_general(
        a, b, (((1,), (1,)), ((), ())), preferred_element_type=F32
    )
    head_grad = (dot(grad, feats_own) + dot(grad_peer, feats_peer)).astype(BF)
    first = collect([first[k] for k in range(4)], "x")
    second = collect([second[k] for k in range(4)], "y")
    line = jnp.concatenate([first, second], axis=1).reshape(8, cols, tokens)
    line = lax.all_to_all(line, ("zh", "t"), 0, 0)
    line, head_grad = lax.optimization_barrier((line, head_grad))
    line = jnp.sum(line, axis=0)
    return (line.astype(BF).T, head_grad, token_loss)


def solution(mesh):
    fine = Mesh(mesh.devices.reshape(4, 2, 4, 4, 2), ("x", "zh", "y", "t", "dp"))
    return jax.shard_map(
        per_device,
        mesh=fine,
        in_specs=(P("dp", SECTIONS), P(SECTIONS, "dp"), P("dp"), P("dp")),
        out_specs=(P("dp", SECTIONS), P(SECTIONS, "dp"), P("dp")),
        check_vma=False,
    )
```

time: 2160 us -> 153 us (0.07)
  waiting for transfers between devices: 1420 us -> 44.6 us
  blocking collectives: 682 us -> 38.7 us
  starting transfers between devices: 0.16 us -> 38.2 us
  matrix products: 30.8 us -> 6.32 us
    unnamed x6 -> x0, waiting for transfers between devices: 730 us -> none
    all_gather x2 -> x0, waiting for transfers between devices: 686 us -> none  [the longest x1 652 us: per_device(): features = lax.all_gather(hidden, ('pipe', 'tensor'), axis=1, tiled=True)]
    psum x1 -> x0, blocking collectives: 342 us -> none  [per_device(): lax.psum((jnp.sum(shifted_exp, axis=0), local_picked), ('pipe', 'tensor'))]
    pmax x1 -> x0, blocking collectives: 340 us -> none  [per_device(): row_peak = lax.pmax(jnp.max(logits, axis=0), ('pipe', 'tensor'))]
    ppermute x0 -> x28, waiting for transfers between devices: none -> 39.8 us  [the longest x12 18.1 us: collect(): got = [lax.ppermute(blocks[k], axis, paired(4, k)) for k in (2, 1, 3)]]
    all_to_all x0 -> x2, blocking collectives: none -> 38.7 us  [share(): lax.all_to_all(jnp.broadcast_to(block[None], (n,) + block.shape), axes, 0...]
    ppermute x0 -> x28, starting transfers between devices: none -> 33.8 us  [the longest x12 16.6 us: spread(): got = {k: lax.ppermute(block, axis, paired(4, k)) for k in (2, 1, 3)}]
  transfers between devices with their start and end apart: 4 -> 29, of which waited for: 4 -> 20; matrix products, arithmetic and copies ran while one was open for 1% -> 6% of each run, Pallas kernels for 0% -> 0%
where the time goes in v1:
time: 153 us
  waiting for transfers between devices  44.6 us (29%)
  blocking collectives  38.7 us (25%)
  starting transfers between devices  38.2 us (25%)
  Pallas kernels  19.5 us (13%)
  matrix products  6.32 us (4%)
  other arithmetic  2.85 us (2%)
  local copies, waits for them, and re-layouts  1.89 us (1%)
    all_to_all x2, blocking collectives, share(): lax.all_to_all(jnp.broadcast_to(block[None], (n,) + block.shape), axes, 0...  38.7 us
    ppermute x12, waiting for transfers between devices, collect(): got = [lax.ppermute(blocks[k], axis, paired(4, k)) for k in (2, 1, 3)]  18.1 us
    ppermute x12, waiting for transfers between devices, spread(): got = {k: lax.ppermute(block, axis, paired(4, k)) for k in (2, 1, 3)}  16.9 us
    ppermute x12, starting transfers between devices, spread(): got = {k: lax.ppermute(block, axis, paired(4, k)) for k in (2, 1, 3)}  16.6 us
    ppermute x12, starting transfers between devices, collect(): got = [lax.ppermute(blocks[k], axis, paired(4, k)) for k in (2, 1, 3)]  14.3 us
    pallas_call x1, Pallas kernels, per_device(): pl.pallas_call(logits_kernel, in_specs=[SMEM] + [HBM] * 2 + [VMEM] * 9, o...  11.3 us
    pallas_call x1, Pallas kernels, per_device(): pl.pallas_call(grad_kernel, in_specs=[SMEM] + [HBM] * 2 + [VMEM] * 4, out...  8.14 us
    dot_general x2, matrix products, per_device(): lax.dot_general(a, b, (((1,), (1,)), ((), ())), preferred_element_type=F32)  6.32 us
  transfers between devices with their start and end apart: 29, of which 20 were waited for; matrix products, arithmetic and copies ran while one was open for 6% of the time, Pallas kernels for 0%

profile of v1, /device:TPU:8, one launch (start us, length us, event | category | flops | bytes accessed | tf_op | source)
XLA Modules:
  0.0 152.9 jit_solution(12189713566529773403)
XLA Ops:
  0.6 0.1 collective-permute-start.6
  0.7 0.7 broadcast_in_dim.8
  1.5 18.7 %all_to_all.15 = bf16[8,40,256]{2,1,0:T(8,128)(2,1)S(1)} all-to-all(bf16[8,40,256]{2,1,0:T(8,128)(2,1)S(1)} %broadcast_in_dim.8), channel_id=1, replica_groups=mesh['x'=4,'zh'=2,'y'=4,'t'=4,'dp'=2] {'zh','t'}, dimensions={0} | all-to-all | bytes 327680 | tf_op jit(solution)/shard_map/all_to_all | solution.py:36
  20.2 2.8 %collective-permute-start.2 = (bf16[2,80,256]{2,1,0:T(8,128)(2,1)S(1)}, bf16[2,80,256]{2,1,0:T(8,128)(2,1)S(1)}, u32[]{:S(2)}, u32[]{:S(2)}) collective-permute-start(bf16[2,80,256]{2,1,0:T(8,128)(2,1)S(1)} %get-tuple-element.63), channel_id=1, source_target_pairs={{0,192},{64,128},{128,64},{192,0},{1,193},{65,129},{129,65},{193,1... | collective-permute-start | bytes 245768 | tf_op jit(solution)/shard_map/ppermute | solution.py:21
  23.0 0.8 collective-permute-start.1
  23.8 0.5 collective-permute-start
  24.4 1.6 %collective-permute-start.5 = (bf16[2,80,256]{2,1,0:T(8,128)(2,1)S(1)}, bf16[2,80,256]{2,1,0:T(8,128)(2,1)S(1)}, u32[]{:S(2)}, u32[]{:S(2)}) collective-permute-start(bf16[2,80,256]{2,1,0:T(8,128)(2,1)S(1)} %get-tuple-element.64), channel_id=1, source_target_pairs={{0,24},{8,16},{16,8},{24,0},{1,25},{9,17},{17,9},{25,1},{2,26},{10... | collective-permute-start | bytes 245768 | tf_op jit(solution)/shard_map/ppermute | solution.py:21
  26.0 2.3 %collective-permute-start.4 = (bf16[2,80,256]{2,1,0:T(8,128)(2,1)S(1)}, bf16[2,80,256]{2,1,0:T(8,128)(2,1)S(1)}, u32[]{:S(2)}, u32[]{:S(2)}) collective-permute-start(bf16[2,80,256]{2,1,0:T(8,128)(2,1)S(1)} %get-tuple-element.64), channel_id=1, source_target_pairs={{0,16},{8,24},{16,0},{24,8},{1,17},{9,25},{17,1},{25,9},{2,18},{10... | collective-permute-start | bytes 245768 | tf_op jit(solution)/shard_map/ppermute | solution.py:21
  28.2 0.7 collective-permute-done.1
  29.0 0.6 collective-permute-start.3
  29.7 0.1 collective-permute-done.5
  29.7 2.3 %collective-permute-done.4 = bf16[2,80,256]{2,1,0:T(8,128)(2,1)S(1)} collective-permute-done((bf16[2,80,256]{2,1,0:T(8,128)(2,1)S(1)}, bf16[2,80,256]{2,1,0:T(8,128)(2,1)S(1)}, u32[]{:S(2)}, u32[]{:S(2)}) %collective-permute-start.4) | collective-permute-done | bytes 81952 | tf_op jit(solution)/shard_map/ppermute | solution.py:21
  32.0 1.4 collective-permute-done.3
  33.5 0.0 collective-permute-done.6.other_far
  33.5 0.0 copy-start.3
  33.5 1.7 %collective-permute-start.9 = (bf16[4,2,80,256]{3,2,1,0:T(8,128)(2,1)S(1)}, bf16[4,2,80,256]{3,2,1,0:T(8,128)(2,1)S(1)}, u32[]{:S(2)}, u32[]{:S(2)}) collective-permute-start(bf16[4,2,80,256]{3,2,1,0:T(8,128)(2,1)S(1)} %pad_maximum_fusion.a0), channel_id=1, source_target_pairs={{0,24},{8,16},{16,8},{24,0},{1,25},{9,17},{17,9},{25,1},{2,26},{10... | collective-permute-start | bytes 983048 | tf_op jit(solution)/shard_map/ppermute | solution.py:21
  35.2 1.1 collective-permute-start.8
  36.3 1.4 collective-permute-start.7
  37.7 3.1 %collective-permute-start.12 = (bf16[4,2,80,256]{3,2,1,0:T(8,128)(2,1)S(1)}, bf16[4,2,80,256]{3,2,1,0:T(8,128)(2,1)S(1)}, u32[]{:S(2)}, u32[]{:S(2)}) collective-permute-start(bf16[4,2,80,256]{3,2,1,0:T(8,128)(2,1)S(1)} %pad_maximum_fusion.1.b0), channel_id=1, source_target_pairs={{0,192},{64,128},{128,64},{192,0},{1,193},{65,129},{129,65},{193,1... | collective-permute-start | bytes 983048 | tf_op jit(solution)/shard_map/ppermute | solution.py:21
  40.8 6.0 %collective-permute-done.9.a3 = bf16[4,2,80,256]{3,2,1,0:T(8,128)(2,1)S(1)} collective-permute-done((bf16[4,2,80,256]{3,2,1,0:T(8,128)(2,1)S(1)}, bf16[4,2,80,256]{3,2,1,0:T(8,128)(2,1)S(1)}, u32[]{:S(2)}, u32[]{:S(2)}) %collective-permute-start.9) | collective-permute-done | bytes 327712 | tf_op jit(solution)/shard_map/ppermute | solution.py:21
  46.7 0.7 collective-permute-start.10
  47.4 0.1 pad_add_fusion.pos
  47.5 1.1 collective-permute-done.7.a1
  48.7 2.9 %collective-permute-done.12.b3 = bf16[4,2,80,256]{3,2,1,0:T(8,128)(2,1)S(1)} collective-permute-done((bf16[4,2,80,256]{3,2,1,0:T(8,128)(2,1)S(1)}, bf16[4,2,80,256]{3,2,1,0:T(8,128)(2,1)S(1)}, u32[]{:S(2)}, u32[]{:S(2)}) %collective-permute-start.12) | collective-permute-done | bytes 327712 | tf_op jit(solution)/shard_map/ppermute | solution.py:21
  51.5 0.0 collective-permute-done.11.b2
  51.5 2.4 %collective-permute-done.10.b1 = bf16[4,2,80,256]{3,2,1,0:T(8,128)(2,1)S(1)} collective-permute-done((bf16[4,2,80,256]{3,2,1,0:T(8,128)(2,1)S(1)}, bf16[4,2,80,256]{3,2,1,0:T(8,128)(2,1)S(1)}, u32[]{:S(2)}, u32[]{:S(2)}) %collective-permute-start.10) | collective-permute-done | bytes 327712 | tf_op jit(solution)/shard_map/ppermute | solution.py:21
  53.9 11.3 %logits.1 = (f32[1187,256]{1,0:T(8,128)S(1)}, f32[3,256]{1,0:T(4,128)S(1)}, bf16[2560,256]{1,0:T(8,128)(2,1)}, bf16[2560,256]{1,0:T(8,128)(2,1)}) custom-call(s32[4]{0:T(128)S(1)} %pad_add_fusion.pos, bf16[1187,2560]{1,0:T(8,128)(2,1)} %own_far.3, bf16[1187,2560]{1,0:T(8,128)(2,1)} %copy-done.3, s32[1,256]{1,0:T(1,128)S(1)} %bitcast.83, ...), custom_call_target="tpu_custom_call" | custom-call | tf_op jit(solution)/shard_map/logits/pallas_call | solution.py:141
  65.3 1.0 copy-done
  66.3 20.0 %all_to_all.16 = f32[64,3,256]{2,1,0:T(4,128)S(1)} all-to-all(f32[64,3,256]{2,1,0:T(4,128)S(1)} %broadcast_in_dim.11), channel_id=1, replica_groups=mesh['x'=4,'zh'=2,'y'=4,'t'=4,'dp'=2] {'x','y','t'}, dimensions={0} | all-to-all | bytes 393216 | tf_op jit(solution)/shard_map/all_to_all | solution.py:36
  86.3 0.2 slice_reduce_fusion.1
  86.5 2.7 %collective-permute-start.13 = (f32[3,256]{1,0:T(4,128)S(1)}, f32[3,256]{1,0:T(4,128)S(1)}, u32[]{:S(2)}, u32[]{:S(2)}) collective-permute-start(f32[3,256]{1,0:T(4,128)S(1)} %pad_maximum_fusion.3), channel_id=1, source_target_pairs={{0,32},{32,0},{1,33},{33,1},{2,34},{34,2},{3,35},{35,3},{4,36},{36... | collective-permute-start | bytes 9224 | tf_op jit(solution)/shard_map/ppermute | solution.py:159
  89.3 4.9 %collective-permute-done.13 = f32[3,256]{1,0:T(4,128)S(1)} collective-permute-done((f32[3,256]{1,0:T(4,128)S(1)}, f32[3,256]{1,0:T(4,128)S(1)}, u32[]{:S(2)}, u32[]{:S(2)}) %collective-permute-start.13) | collective-permute-done | bytes 3104 | tf_op jit(solution)/shard_map/ppermute | solution.py:159
  94.2 8.1 %grads.1 = (bf16[1187,256]{1,0:T(8,128)(2,1)S(1)}, bf16[4,2,80,256]{3,2,1,0:T(8,128)(2,1)S(1)}, bf16[4,2,80,256]{3,2,1,0:T(8,128)(2,1)S(1)}, bf16[4,2,80,256]{3,...) custom-call(s32[4]{0:T(128)S(1)} %pad_add_fusion.pos, ...), custom_call_target="tpu_custom_call" | custom-call | tf_op jit(solution)/shard_map/grads/pallas_call | solution.py:162
  102.4 0.8 collective-permute-start.14
  103.2 1.3 collective-permute-start.15
  104.4 2.1 %collective-permute-start.16 = (bf16[4,2,80,256]{3,2,1,0:T(8,128)(2,1)S(1)}, bf16[4,2,80,256]{3,2,1,0:T(8,128)(2,1)S(1)}, u32[]{:S(2)}, u32[]{:S(2)}) collective-permute-start(bf16[4,2,80,256]{3,2,1,0:T(8,128)(2,1)S(1)} %get-tuple-element.36), channel_id=1, source_target_pairs={{0,24},{8,16},{16,8},{24,0},{1,25},{9,17},{17,9},{25,1},{2,26},{10... | collective-permute-start | bytes 983048 | tf_op jit(solution)/shard_map/ppermute | solution.py:27
  106.6 0.6 collective-permute-start.17
  107.2 1.0 collective-permute-start.18
  108.2 4.3 %collective-permute-done.14 = bf16[4,2,80,256]{3,2,1,0:T(8,128)(2,1)S(1)} collective-permute-done((bf16[4,2,80,256]{3,2,1,0:T(8,128)(2,1)S(1)}, bf16[4,2,80,256]{3,2,1,0:T(8,128)(2,1)S(1)}, u32[]{:S(2)}, u32[]{:S(2)}) %collective-permute-start.14) | collective-permute-done | bytes 327712 | tf_op jit(solution)/shard_map/ppermute | solution.py:27
  112.5 0.9 collective-permute-start.19
  113.3 0.6 add_subtract_fusion
  113.9 0.3 collective-permute-done.15
  114.2 1.6 %collective-permute-done.16 = bf16[4,2,80,256]{3,2,1,0:T(8,128)(2,1)S(1)} collective-permute-done((bf16[4,2,80,256]{3,2,1,0:T(8,128)(2,1)S(1)}, bf16[4,2,80,256]{3,2,1,0:T(8,128)(2,1)S(1)}, u32[]{:S(2)}, u32[]{:S(2)}) %collective-permute-start.16) | collective-permute-done | bytes 327712 | tf_op jit(solution)/shard_map/ppermute | solution.py:27
  115.8 0.2 add_convert_fusion.1
  116.0 1.3 collective-permute-done.18
  117.3 4.6 %collective-permute-done.19 = bf16[4,2,80,256]{3,2,1,0:T(8,128)(2,1)S(1)} collective-permute-done((bf16[4,2,80,256]{3,2,1,0:T(8,128)(2,1)S(1)}, bf16[4,2,80,256]{3,2,1,0:T(8,128)(2,1)S(1)}, u32[]{:S(2)}, u32[]{:S(2)}) %collective-permute-start.19) | collective-permute-done | bytes 327712 | tf_op jit(solution)/shard_map/ppermute | solution.py:27
  121.9 0.2 add_convert_fusion
  122.2 0.1 collective-permute-start.20
  122.3 0.6 collective-permute-start.22
  122.9 2.8 %collective-permute-start.21 = (bf16[2,80,256]{2,1,0:T(8,128)(2,1)S(1)}, bf16[2,80,256]{2,1,0:T(8,128)(2,1)S(1)}, u32[]{:S(2)}, u32[]{:S(2)}) collective-permute-start(bf16[2,80,256]{2,1,0:T(8,128)(2,1)S(1)} %get-tuple-element.55), channel_id=1, source_target_pairs={{0,64},{64,0},{128,192},{192,128},{1,65},{65,1},{129,193},{193,129... | collective-permute-start | bytes 245768 | tf_op jit(solution)/shard_map/ppermute | solution.py:27
  125.7 0.0 collective-permute-start.26
  125.8 2.5 %collective-permute-done.20 = bf16[2,80,256]{2,1,0:T(8,128)(2,1)S(1)} collective-permute-done((bf16[2,80,256]{2,1,0:T(8,128)(2,1)S(1)}, bf16[2,80,256]{2,1,0:T(8,128)(2,1)S(1)}, u32[]{:S(2)}, u32[]{:S(2)}) %collective-permute-start.20) | collective-permute-done | bytes 81952 | tf_op jit(solution)/shard_map/ppermute | solution.py:27
  128.3 0.6 collective-permute-done.22
  128.9 2.5 %collective-permute-start.25 = (bf16[2,80,256]{2,1,0:T(8,128)(2,1)S(1)}, bf16[2,80,256]{2,1,0:T(8,128)(2,1)S(1)}, u32[]{:S(2)}, u32[]{:S(2)}) collective-permute-start(bf16[2,80,256]{2,1,0:T(8,128)(2,1)S(1)} %get-tuple-element.57), channel_id=1, source_target_pairs={{0,24},{8,16},{16,8},{24,0},{1,25},{9,17},{17,9},{25,1},{2,26},{10... | collective-permute-start | bytes 245768 | tf_op jit(solution)/shard_map/ppermute | solution.py:27
  131.4 1.6 %collective-permute-start.24 = (bf16[2,80,256]{2,1,0:T(8,128)(2,1)S(1)}, bf16[2,80,256]{2,1,0:T(8,128)(2,1)S(1)}, u32[]{:S(2)}, u32[]{:S(2)}) collective-permute-start(bf16[2,80,256]{2,1,0:T(8,128)(2,1)S(1)} %get-tuple-element.58), channel_id=1, source_target_pairs={{0,8},{8,0},{16,24},{24,16},{1,9},{9,1},{17,25},{25,17},{2,10},{10... | collective-permute-start | bytes 245768 | tf_op jit(solution)/shard_map/ppermute | solution.py:27
  133.0 1.3 collective-permute-done.23
  134.3 0.4 collective-permute-done.25
  134.7 1.1 collective-permute-done.24
  135.9 0.8 pad_maximum_fusion.2
  136.7 4.4 %all-to-all-start.2 = ((f32[8,40,256]{2,1,0:T(8,128)}), f32[8,40,256]{2,1,0:T(8,128)S(1)}, u32[]{:S(2)}, u32[]{:S(2)}) async-start(f32[8,40,256]{2,1,0:T(8,128)} %bitcast.36), calls=%async_computation.2 | async-start | bytes 655360 | tf_op jit(solution)/shard_map/all_to_all | solution.py:189
  141.1 1.8 %fusion.17 = f32[1187,2560]{1,0:T(8,128)S(1)} fusion(bf16[1187,256]{1,0:T(8,128)(2,1)S(1)} %collective-permute-done.26, bf16[2560,256]{1,0:T(8,128)(2,1)S(1)} %collective-permute-done.27), kind=kOutput, calls=%fused_computation.48 | convolution fusion | flops 1555824640 | bytes 14073344 | tf_op jit(solution)/shard_map/dot_general | solution.py:182
  142.9 4.5 %fusion = bf16[1187,2560]{1,0:T(8,128)(2,1)} fusion(f32[1187,2560]{1,0:T(8,128)S(1)} %fusion.17, bf16[1187,256]{1,0:T(8,128)(2,1)S(1)} %get-tuple-element.44, bf16[2560,256]{1,0:T(8,128)(2,1)S(1)} %copy-done.4), kind=kOutput, calls=%fused_computation.1 | convolution fusion | flops 1561902080 | bytes 20150784 | tf_op jit(solution)/shard_map/dot_general | solution.py:182
  147.4 4.8 %all-to-all-done.2 = f32[8,40,256]{2,1,0:T(8,128)S(1)} async-done(((f32[8,40,256]{2,1,0:T(8,128)}), f32[8,40,256]{2,1,0:T(8,128)S(1)}, u32[]{:S(2)}, u32[]{:S(2)}) %all-to-all-start.2) | async-done | bytes 327712 | tf_op jit(solution)/shard_map/all_to_all | solution.py:189
  152.2 0.6 reduce_sum.49
  (33 shorter events, 0.4 us)
Async XLA Ops:
  0.6 53.3 %copy-start.1 = (s32[256]{0:T(256)S(1)}, s32[256]{0:T(256)}, u32[]{:S(2)}) copy-start(s32[256]{0:T(256)} %param.6) | copy-start | bytes 3076
  0.6 32.8 %collective-permute-start.6 = (bf16[1187,2560]{1,0:T(8,128)(2,1)}, bf16[1187,2560]{1,0:T(8,128)(2,1)S(1)}, u32[]{:S(2)}, u32[]{:S(2)}) collective-permute-start(bf16[1187,2560]{1,0:T(8,128)(2,1)} %own_far.3), channel_id=1, source_target_pairs={{0,1},{1,0},{2,3},{3,2},{4,5},{5,4},{6,7},{7,6},{8,9},{9,8},{10,11... | collective-permute-start | bytes 18232328 | tf_op jit(solution)/shard_map/ppermute | solution.py:125
  20.2 5.8 %collective-permute-start.2 = (bf16[2,80,256]{2,1,0:T(8,128)(2,1)S(1)}, bf16[2,80,256]{2,1,0:T(8,128)(2,1)S(1)}, u32[]{:S(2)}, u32[]{:S(2)}) collective-permute-start(bf16[2,80,256]{2,1,0:T(8,128)(2,1)S(1)} %get-tuple-element.63), channel_id=1, source_target_pairs={{0,192},{64,128},{128,64},{192,0},{1,193},{65,129},{129,65},{193,1... | collective-permute-start | bytes 245768 | tf_op jit(solution)/shard_map/ppermute | solution.py:21
  23.0 5.9 %collective-permute-start.1 = (bf16[2,80,256]{2,1,0:T(8,128)(2,1)S(1)}, bf16[2,80,256]{2,1,0:T(8,128)(2,1)S(1)}, u32[]{:S(2)}, u32[]{:S(2)}) collective-permute-start(bf16[2,80,256]{2,1,0:T(8,128)(2,1)S(1)} %get-tuple-element.63), channel_id=1, source_target_pairs={{0,128},{64,192},{128,0},{192,64},{1,129},{65,193},{129,1},{193,65... | collective-permute-start | bytes 245768 | tf_op jit(solution)/shard_map/ppermute | solution.py:21
  23.8 5.8 %collective-permute-start = (bf16[2,80,256]{2,1,0:T(8,128)(2,1)S(1)}, bf16[2,80,256]{2,1,0:T(8,128)(2,1)S(1)}, u32[]{:S(2)}, u32[]{:S(2)}) collective-permute-start(bf16[2,80,256]{2,1,0:T(8,128)(2,1)S(1)} %get-tuple-element.63), channel_id=1, source_target_pairs={{0,64},{64,0},{128,192},{192,128},{1,65},{65,1},{129,193},{193,129... | collective-permute-start | bytes 245768 | tf_op jit(solution)/shard_map/ppermute | solution.py:21
  24.4 5.3 %collective-permute-start.5 = (bf16[2,80,256]{2,1,0:T(8,128)(2,1)S(1)}, bf16[2,80,256]{2,1,0:T(8,128)(2,1)S(1)}, u32[]{:S(2)}, u32[]{:S(2)}) collective-permute-start(bf16[2,80,256]{2,1,0:T(8,128)(2,1)S(1)} %get-tuple-element.64), channel_id=1, source_target_pairs={{0,24},{8,16},{16,8},{24,0},{1,25},{9,17},{17,9},{25,1},{2,26},{10... | collective-permute-start | bytes 245768 | tf_op jit(solution)/shard_map/ppermute | solution.py:21
  26.0 6.0 %collective-permute-start.4 = (bf16[2,80,256]{2,1,0:T(8,128)(2,1)S(1)}, bf16[2,80,256]{2,1,0:T(8,128)(2,1)S(1)}, u32[]{:S(2)}, u32[]{:S(2)}) collective-permute-start(bf16[2,80,256]{2,1,0:T(8,128)(2,1)S(1)} %get-tuple-element.64), channel_id=1, source_target_pairs={{0,16},{8,24},{16,0},{24,8},{1,17},{9,25},{17,1},{25,9},{2,18},{10... | collective-permute-start | bytes 245768 | tf_op jit(solution)/shard_map/ppermute | solution.py:21
  29.0 4.4 %collective-permute-start.3 = (bf16[2,80,256]{2,1,0:T(8,128)(2,1)S(1)}, bf16[2,80,256]{2,1,0:T(8,128)(2,1)S(1)}, u32[]{:S(2)}, u32[]{:S(2)}) collective-permute-start(bf16[2,80,256]{2,1,0:T(8,128)(2,1)S(1)} %get-tuple-element.64), channel_id=1, source_target_pairs={{0,8},{8,0},{16,24},{24,16},{1,9},{9,1},{17,25},{25,17},{2,10},{10... | collective-permute-start | bytes 245768 | tf_op jit(solution)/shard_map/ppermute | solution.py:21
  33.5 13.2 %copy-start.3 = (bf16[1187,2560]{1,0:T(8,128)(2,1)}, bf16[1187,2560]{1,0:T(8,128)(2,1)S(1)}, u32[]{:S(2)}) copy-start(bf16[1187,2560]{1,0:T(8,128)(2,1)S(1)} %collective-permute-done.6.other_far) | copy-start | bytes 18232324
  33.5 13.2 %collective-permute-start.9 = (bf16[4,2,80,256]{3,2,1,0:T(8,128)(2,1)S(1)}, bf16[4,2,80,256]{3,2,1,0:T(8,128)(2,1)S(1)}, u32[]{:S(2)}, u32[]{:S(2)}) collective-permute-start(bf16[4,2,80,256]{3,2,1,0:T(8,128)(2,1)S(1)} %pad_maximum_fusion.a0), channel_id=1, source_target_pairs={{0,24},{8,16},{16,8},{24,0},{1,25},{9,17},{17,9},{25,1},{2,26},{10... | collective-permute-start | bytes 983048 | tf_op jit(solution)/shard_map/ppermute | solution.py:21
  35.2 12.4 %collective-permute-start.8 = (bf16[4,2,80,256]{3,2,1,0:T(8,128)(2,1)S(1)}, bf16[4,2,80,256]{3,2,1,0:T(8,128)(2,1)S(1)}, u32[]{:S(2)}, u32[]{:S(2)}) collective-permute-start(bf16[4,2,80,256]{3,2,1,0:T(8,128)(2,1)S(1)} %pad_maximum_fusion.a0), channel_id=1, source_target_pairs={{0,16},{8,24},{16,0},{24,8},{1,17},{9,25},{17,1},{25,9},{2,18},{10... | collective-permute-start | bytes 983048 | tf_op jit(solution)/shard_map/ppermute | solution.py:21
  36.3 12.4 %collective-permute-start.7 = (bf16[4,2,80,256]{3,2,1,0:T(8,128)(2,1)S(1)}, bf16[4,2,80,256]{3,2,1,0:T(8,128)(2,1)S(1)}, u32[]{:S(2)}, u32[]{:S(2)}) collective-permute-start(bf16[4,2,80,256]{3,2,1,0:T(8,128)(2,1)S(1)} %pad_maximum_fusion.a0), channel_id=1, source_target_pairs={{0,8},{8,0},{16,24},{24,16},{1,9},{9,1},{17,25},{25,17},{2,10},{10... | collective-permute-start | bytes 983048 | tf_op jit(solution)/shard_map/ppermute | solution.py:21
  37.7 13.8 %collective-permute-start.12 = (bf16[4,2,80,256]{3,2,1,0:T(8,128)(2,1)S(1)}, bf16[4,2,80,256]{3,2,1,0:T(8,128)(2,1)S(1)}, u32[]{:S(2)}, u32[]{:S(2)}) collective-permute-start(bf16[4,2,80,256]{3,2,1,0:T(8,128)(2,1)S(1)} %pad_maximum_fusion.1.b0), channel_id=1, source_target_pairs={{0,192},{64,128},{128,64},{192,0},{1,193},{65,129},{129,65},{193,1... | collective-permute-start | bytes 983048 | tf_op jit(solution)/shard_map/ppermute | solution.py:21
  40.8 10.8 %collective-permute-start.11 = (bf16[4,2,80,256]{3,2,1,0:T(8,128)(2,1)S(1)}, bf16[4,2,80,256]{3,2,1,0:T(8,128)(2,1)S(1)}, u32[]{:S(2)}, u32[]{:S(2)}) collective-permute-start(bf16[4,2,80,256]{3,2,1,0:T(8,128)(2,1)S(1)} %pad_maximum_fusion.1.b0), channel_id=1, source_target_pairs={{0,128},{64,192},{128,0},{192,64},{1,129},{65,193},{129,1},{193,65... | collective-permute-start | bytes 983048 | tf_op jit(solution)/shard_map/ppermute | solution.py:21
  46.7 7.2 %collective-permute-start.10 = (bf16[4,2,80,256]{3,2,1,0:T(8,128)(2,1)S(1)}, bf16[4,2,80,256]{3,2,1,0:T(8,128)(2,1)S(1)}, u32[]{:S(2)}, u32[]{:S(2)}) collective-permute-start(bf16[4,2,80,256]{3,2,1,0:T(8,128)(2,1)S(1)} %pad_maximum_fusion.1.b0), channel_id=1, source_target_pairs={{0,64},{64,0},{128,192},{192,128},{1,65},{65,1},{129,193},{193,129... | collective-permute-start | bytes 983048 | tf_op jit(solution)/shard_map/ppermute | solution.py:21
  65.3 1.0 copy-start
  66.3 27.9 %copy-start.2 = (f32[256]{0:T(256)S(1)}, f32[256]{0:T(256)}, u32[]{:S(2)}) copy-start(f32[256]{0:T(256)} %param.7) | copy-start | bytes 3076
  86.5 7.6 %collective-permute-start.13 = (f32[3,256]{1,0:T(4,128)S(1)}, f32[3,256]{1,0:T(4,128)S(1)}, u32[]{:S(2)}, u32[]{:S(2)}) collective-permute-start(f32[3,256]{1,0:T(4,128)S(1)} %pad_maximum_fusion.3), channel_id=1, source_target_pairs={{0,32},{32,0},{1,33},{33,1},{2,34},{34,2},{3,35},{35,3},{4,36},{36... | collective-permute-start | bytes 9224 | tf_op jit(solution)/shard_map/ppermute | solution.py:159
  102.4 10.1 %collective-permute-start.14 = (bf16[4,2,80,256]{3,2,1,0:T(8,128)(2,1)S(1)}, bf16[4,2,80,256]{3,2,1,0:T(8,128)(2,1)S(1)}, u32[]{:S(2)}, u32[]{:S(2)}) collective-permute-start(bf16[4,2,80,256]{3,2,1,0:T(8,128)(2,1)S(1)} %get-tuple-element.34), channel_id=1, source_target_pairs={{0,16},{8,24},{16,0},{24,8},{1,17},{9,25},{17,1},{25,9},{2,18},{10... | collective-permute-start | bytes 983048 | tf_op jit(solution)/shard_map/ppermute | solution.py:27
  103.2 11.1 %collective-permute-start.15 = (bf16[4,2,80,256]{3,2,1,0:T(8,128)(2,1)S(1)}, bf16[4,2,80,256]{3,2,1,0:T(8,128)(2,1)S(1)}, u32[]{:S(2)}, u32[]{:S(2)}) collective-permute-start(bf16[4,2,80,256]{3,2,1,0:T(8,128)(2,1)S(1)} %get-tuple-element.35), channel_id=1, source_target_pairs={{0,8},{8,0},{16,24},{24,16},{1,9},{9,1},{17,25},{25,17},{2,10},{10... | collective-permute-start | bytes 983048 | tf_op jit(solution)/shard_map/ppermute | solution.py:27
  104.4 11.4 %collective-permute-start.16 = (bf16[4,2,80,256]{3,2,1,0:T(8,128)(2,1)S(1)}, bf16[4,2,80,256]{3,2,1,0:T(8,128)(2,1)S(1)}, u32[]{:S(2)}, u32[]{:S(2)}) collective-permute-start(bf16[4,2,80,256]{3,2,1,0:T(8,128)(2,1)S(1)} %get-tuple-element.36), channel_id=1, source_target_pairs={{0,24},{8,16},{16,8},{24,0},{1,25},{9,17},{17,9},{25,1},{2,26},{10... | collective-permute-start | bytes 983048 | tf_op jit(solution)/shard_map/ppermute | solution.py:27
  106.6 9.5 %collective-permute-start.17 = (bf16[4,2,80,256]{3,2,1,0:T(8,128)(2,1)S(1)}, bf16[4,2,80,256]{3,2,1,0:T(8,128)(2,1)S(1)}, u32[]{:S(2)}, u32[]{:S(2)}) collective-permute-start(bf16[4,2,80,256]{3,2,1,0:T(8,128)(2,1)S(1)} %get-tuple-element.38), channel_id=1, source_target_pairs={{0,128},{64,192},{128,0},{192,64},{1,129},{65,193},{129,1},{193,65... | collective-permute-start | bytes 983048 | tf_op jit(solution)/shard_map/ppermute | solution.py:27
  107.2 10.1 %collective-permute-start.18 = (bf16[4,2,80,256]{3,2,1,0:T(8,128)(2,1)S(1)}, bf16[4,2,80,256]{3,2,1,0:T(8,128)(2,1)S(1)}, u32[]{:S(2)}, u32[]{:S(2)}) collective-permute-start(bf16[4,2,80,256]{3,2,1,0:T(8,128)(2,1)S(1)} %get-tuple-element.39), channel_id=1, source_target_pairs={{0,64},{64,0},{128,192},{192,128},{1,65},{65,1},{129,193},{193,129... | collective-permute-start | bytes 983048 | tf_op jit(solution)/shard_map/ppermute | solution.py:27
  112.5 9.5 %collective-permute-start.19 = (bf16[4,2,80,256]{3,2,1,0:T(8,128)(2,1)S(1)}, bf16[4,2,80,256]{3,2,1,0:T(8,128)(2,1)S(1)}, u32[]{:S(2)}, u32[]{:S(2)}) collective-permute-start(bf16[4,2,80,256]{3,2,1,0:T(8,128)(2,1)S(1)} %get-tuple-element.40), channel_id=1, source_target_pairs={{0,192},{64,128},{128,64},{192,0},{1,193},{65,129},{129,65},{193,1... | collective-permute-start | bytes 983048 | tf_op jit(solution)/shard_map/ppermute | solution.py:27
  114.2 26.8 %collective-permute-start.27 = (bf16[2560,256]{1,0:T(8,128)(2,1)}, bf16[2560,256]{1,0:T(8,128)(2,1)S(1)}, u32[]{:S(2)}, u32[]{:S(2)}) collective-permute-start(bf16[2560,256]{1,0:T(8,128)(2,1)} %get-tuple-element.46), channel_id=1, source_target_pairs={{0,1},{1,0},{2,3},{3,2},{4,5},{5,4},{6,7},{7,6},{8,9},{9,8},{10,11... | collective-permute-start | bytes 3932168 | tf_op jit(solution)/shard_map/ppermute | solution.py:158
  122.2 6.1 %collective-permute-start.20 = (bf16[2,80,256]{2,1,0:T(8,128)(2,1)S(1)}, bf16[2,80,256]{2,1,0:T(8,128)(2,1)S(1)}, u32[]{:S(2)}, u32[]{:S(2)}) collective-permute-start(bf16[2,80,256]{2,1,0:T(8,128)(2,1)S(1)} %get-tuple-element.53), channel_id=1, source_target_pairs={{0,128},{64,192},{128,0},{192,64},{1,129},{65,193},{129,1},{193,65... | collective-permute-start | bytes 245768 | tf_op jit(solution)/shard_map/ppermute | solution.py:27
  122.3 6.6 %collective-permute-start.22 = (bf16[2,80,256]{2,1,0:T(8,128)(2,1)S(1)}, bf16[2,80,256]{2,1,0:T(8,128)(2,1)S(1)}, u32[]{:S(2)}, u32[]{:S(2)}) collective-permute-start(bf16[2,80,256]{2,1,0:T(8,128)(2,1)S(1)} %get-tuple-element.54), channel_id=1, source_target_pairs={{0,192},{64,128},{128,64},{192,0},{1,193},{65,129},{129,65},{193,1... | collective-permute-start | bytes 245768 | tf_op jit(solution)/shard_map/ppermute | solution.py:27
  122.9 8.5 %collective-permute-start.21 = (bf16[2,80,256]{2,1,0:T(8,128)(2,1)S(1)}, bf16[2,80,256]{2,1,0:T(8,128)(2,1)S(1)}, u32[]{:S(2)}, u32[]{:S(2)}) collective-permute-start(bf16[2,80,256]{2,1,0:T(8,128)(2,1)S(1)} %get-tuple-element.55), channel_id=1, source_target_pairs={{0,64},{64,0},{128,192},{192,128},{1,65},{65,1},{129,193},{193,129... | collective-permute-start | bytes 245768 | tf_op jit(solution)/shard_map/ppermute | solution.py:27
  125.7 15.3 %collective-permute-start.26 = (bf16[1187,256]{1,0:T(8,128)(2,1)S(1)}, bf16[1187,256]{1,0:T(8,128)(2,1)S(1)}, u32[]{:S(2)}, u32[]{:S(2)}) collective-permute-start(bf16[1187,256]{1,0:T(8,128)(2,1)S(1)} %get-tuple-element.44), channel_id=1, source_target_pairs={{0,1},{1,0},{2,3},{3,2},{4,5},{5,4},{6,7},{7,6},{8,9},{9,8},{10,11... | collective-permute-start | bytes 1823240 | tf_op jit(solution)/shard_map/ppermute | solution.py:181
  128.3 6.1 %collective-permute-start.23 = (bf16[2,80,256]{2,1,0:T(8,128)(2,1)S(1)}, bf16[2,80,256]{2,1,0:T(8,128)(2,1)S(1)}, u32[]{:S(2)}, u32[]{:S(2)}) collective-permute-start(bf16[2,80,256]{2,1,0:T(8,128)(2,1)S(1)} %get-tuple-element.56), channel_id=1, source_target_pairs={{0,16},{8,24},{16,0},{24,8},{1,17},{9,25},{17,1},{25,9},{2,18},{10... | collective-permute-start | bytes 245768 | tf_op jit(solution)/shard_map/ppermute | solution.py:27
  128.9 5.8 %collective-permute-start.25 = (bf16[2,80,256]{2,1,0:T(8,128)(2,1)S(1)}, bf16[2,80,256]{2,1,0:T(8,128)(2,1)S(1)}, u32[]{:S(2)}, u32[]{:S(2)}) collective-permute-start(bf16[2,80,256]{2,1,0:T(8,128)(2,1)S(1)} %get-tuple-element.57), channel_id=1, source_target_pairs={{0,24},{8,16},{16,8},{24,0},{1,25},{9,17},{17,9},{25,1},{2,26},{10... | collective-permute-start | bytes 245768 | tf_op jit(solution)/shard_map/ppermute | solution.py:27
  131.4 4.4 %collective-permute-start.24 = (bf16[2,80,256]{2,1,0:T(8,128)(2,1)S(1)}, bf16[2,80,256]{2,1,0:T(8,128)(2,1)S(1)}, u32[]{:S(2)}, u32[]{:S(2)}) collective-permute-start(bf16[2,80,256]{2,1,0:T(8,128)(2,1)S(1)} %get-tuple-element.58), channel_id=1, source_target_pairs={{0,8},{8,0},{16,24},{24,16},{1,9},{9,1},{17,25},{25,17},{2,10},{10... | collective-permute-start | bytes 245768 | tf_op jit(solution)/shard_map/ppermute | solution.py:27
  136.7 15.6 %all-to-all-start.2 = ((f32[8,40,256]{2,1,0:T(8,128)}), f32[8,40,256]{2,1,0:T(8,128)S(1)}, u32[]{:S(2)}, u32[]{:S(2)}) async-start(f32[8,40,256]{2,1,0:T(8,128)} %bitcast.36), calls=%async_computation.2 | async-start | bytes 655360 | tf_op jit(solution)/shard_map/all_to_all | solution.py:189
  141.0 1.8 %copy-start.4 = (bf16[2560,256]{1,0:T(8,128)(2,1)S(1)}, bf16[2560,256]{1,0:T(8,128)(2,1)}, u32[]{:S(2)}) copy-start(bf16[2560,256]{1,0:T(8,128)(2,1)} %get-tuple-element.45) | copy-start | bytes 3932164

commit v2 on v1

--- a/solution.py
+++ b/solution.py
@@ -61,12 +61,13 @@
 
 
 def fetch(own_far, other_far, own, other, sems):
-    copies = [
-        pltpu.make_async_copy(own_far, own, sems.at[0]),
-        pltpu.make_async_copy(other_far, other, sems.at[1]),
-    ]
-    for copy in copies:
-        copy.start()
+    width = own.shape[1] // 2
+    copies = []
+    for j in range(4):
+        far, near = (own_far, own) if j < 2 else (other_far, other)
+        span = pl.ds((j % 2) * width, width)
+        copies.append(pltpu.make_async_copy(far.at[:, span], near.at[:, span], sems.at[j]))
+        copies[-1].start()
     return copies
 
 
@@ -80,9 +81,13 @@
     firsts, seconds = (a0, a1, a2, a3), (b0, b1, b2, b3)
     each_piece(pos, a0.shape[2], firsts, seconds, feats_own, feats_other, place)
     copies[0].wait()
+    copies[1].wait()
     logits[...] = jnp.dot(own[...], feats_own[...], preferred_element_type=F32)
-    copies[1].wait()
-    logits[...] += jnp.dot(other[...], feats_other[...], preferred_element_type=F32)
+    width = own.shape[1] // 2
+    for j in range(2):
+        copies[2 + j].wait()
+        span = slice(j * width, (j + 1) * width)
+        logits[...] += jnp.dot(other[:, span], feats_other[span], preferred_element_type=F32)
     value = logits[...]
     rows = lax.broadcasted_iota(jnp.int32, value.shape, 0) + pos[3]
     peak = jnp.max(value, axis=0, keepdims=True)
@@ -103,8 +108,7 @@
     grad_t[...] = result.T.astype(BF)
     width = own.shape[1] // 2
     for j in range(4):
-        if j % 2 == 0:
-            copies[j // 2].wait()
+        copies[j].wait()
         weight, part = (own, part_own) if j < 2 else (other, part_other)
         span = slice((j % 2) * width, (j % 2 + 1) * width)
         piece = jnp.dot(grad_t[...], weight[:, span], preferred_element_type=F32)
@@ -129,8 +133,8 @@
     ).astype(jnp.int32)
     labels = labels[None, :]
     loss_weight = loss_weight[None, :]
-    params = pltpu.CompilerParams(vmem_limit_bytes=50 * 1024 * 1024)
-    weights = [pltpu.VMEM((rows, half), BF)] * 2 + [pltpu.SemaphoreType.DMA((2,))]
+    params = pltpu.CompilerParams(vmem_limit_bytes=42 * 1024 * 1024)
+    weights = [pltpu.VMEM((rows, half), BF)] * 2 + [pltpu.SemaphoreType.DMA((4,))]
 
     line = share(hidden.T, ("zh", "t")).reshape(2, 2, side, tokens)
     first = jnp.stack(spread(line[:, 0], "x"))
@@ -149,7 +153,7 @@
             jax.ShapeDtypeStruct((half, tokens), BF),
         ],
         scratch_shapes=weights,
-        compiler_params=params,
+        compiler_params=pltpu.CompilerParams(vmem_limit_bytes=50 * 1024 * 1024),
         name="logits",
     )(pos, head_weight, weight_other, labels, *first, *second)
 

time: 153 us -> 150 us (0.980)
  Pallas kernels: 19.5 us -> 17.5 us
where the time goes in v2:
time: 150 us
  waiting for transfers between devices  44.6 us (30%)
  blocking collectives  38.9 us (26%)
  starting transfers between devices  38.2 us (25%)
  Pallas kernels  17.5 us (12%)
  matrix products  6.31 us (4%)
  other arithmetic  2.86 us (2%)
    all_to_all x2, blocking collectives, share(): lax.all_to_all(jnp.broadcast_to(block[None], (n,) + block.shape), axes, 0...  38.9 us
    ppermute x12, waiting for transfers between devices, collect(): got = [lax.ppermute(blocks[k], axis, paired(4, k)) for k in (2, 1, 3)]  18.1 us
    ppermute x12, waiting for transfers between devices, spread(): got = {k: lax.ppermute(block, axis, paired(4, k)) for k in (2, 1, 3)}  16.9 us
    ppermute x12, starting transfers between devices, spread(): got = {k: lax.ppermute(block, axis, paired(4, k)) for k in (2, 1, 3)}  16.6 us
    ppermute x12, starting transfers between devices, collect(): got = [lax.ppermute(blocks[k], axis, paired(4, k)) for k in (2, 1, 3)]  14.3 us
    pallas_call x1, Pallas kernels, per_device(): pl.pallas_call(logits_kernel, in_specs=[SMEM] + [HBM] * 2 + [VMEM] * 9, o...  10.8 us
    pallas_call x1, Pallas kernels, per_device(): pl.pallas_call(grad_kernel, in_specs=[SMEM] + [HBM] * 2 + [VMEM] * 4, out...  6.74 us
    dot_general x2, matrix products, per_device(): lax.dot_general(a, b, (((1,), (1,)), ((), ())), preferred_element_type=F32)  6.31 us
  transfers between devices with their start and end apart: 29, of which 20 were waited for; matrix products, arithmetic and copies ran while one was open for 6% of the time, Pallas kernels for 0%

profile of v2, /device:TPU:8, one launch (start us, length us, event | category | flops | bytes accessed | tf_op | source)
XLA Modules:
  0.0 150.1 jit_solution(233179308411622581)
XLA Ops:
  0.6 0.1 collective-permute-start.6
  0.7 0.7 broadcast_in_dim.8
  1.5 18.7 %all_to_all.15 = bf16[8,40,256]{2,1,0:T(8,128)(2,1)S(1)} all-to-all(bf16[8,40,256]{2,1,0:T(8,128)(2,1)S(1)} %broadcast_in_dim.8), channel_id=1, replica_groups=mesh['x'=4,'zh'=2,'y'=4,'t'=4,'dp'=2] {'zh','t'}, dimensions={0} | all-to-all | bytes 327680 | tf_op jit(solution)/shard_map/all_to_all | solution.py:36
  20.2 2.8 %collective-permute-start.2 = (bf16[2,80,256]{2,1,0:T(8,128)(2,1)S(1)}, bf16[2,80,256]{2,1,0:T(8,128)(2,1)S(1)}, u32[]{:S(2)}, u32[]{:S(2)}) collective-permute-start(bf16[2,80,256]{2,1,0:T(8,128)(2,1)S(1)} %get-tuple-element.63), channel_id=1, source_target_pairs={{0,192},{64,128},{128,64},{192,0},{1,193},{65,129},{129,65},{193,1... | collective-permute-start | bytes 245768 | tf_op jit(solution)/shard_map/ppermute | solution.py:21
  23.0 0.8 collective-permute-start.1
  23.8 0.5 collective-permute-start
  24.4 1.6 %collective-permute-start.5 = (bf16[2,80,256]{2,1,0:T(8,128)(2,1)S(1)}, bf16[2,80,256]{2,1,0:T(8,128)(2,1)S(1)}, u32[]{:S(2)}, u32[]{:S(2)}) collective-permute-start(bf16[2,80,256]{2,1,0:T(8,128)(2,1)S(1)} %get-tuple-element.64), channel_id=1, source_target_pairs={{0,24},{8,16},{16,8},{24,0},{1,25},{9,17},{17,9},{25,1},{2,26},{10... | collective-permute-start | bytes 245768 | tf_op jit(solution)/shard_map/ppermute | solution.py:21
  26.0 0.0 collective-permute-done.2
  26.0 2.3 %collective-permute-start.4 = (bf16[2,80,256]{2,1,0:T(8,128)(2,1)S(1)}, bf16[2,80,256]{2,1,0:T(8,128)(2,1)S(1)}, u32[]{:S(2)}, u32[]{:S(2)}) collective-permute-start(bf16[2,80,256]{2,1,0:T(8,128)(2,1)S(1)} %get-tuple-element.64), channel_id=1, source_target_pairs={{0,16},{8,24},{16,0},{24,8},{1,17},{9,25},{17,1},{25,9},{2,18},{10... | collective-permute-start | bytes 245768 | tf_op jit(solution)/shard_map/ppermute | solution.py:21
  28.2 0.7 collective-permute-done.1
  29.0 0.6 collective-permute-start.3
  29.6 0.0 collective-permute-done
  29.7 0.1 collective-permute-done.5
  29.7 2.3 %collective-permute-done.4 = bf16[2,80,256]{2,1,0:T(8,128)(2,1)S(1)} collective-permute-done((bf16[2,80,256]{2,1,0:T(8,128)(2,1)S(1)}, bf16[2,80,256]{2,1,0:T(8,128)(2,1)S(1)}, u32[]{:S(2)}, u32[]{:S(2)}) %collective-permute-start.4) | collective-permute-done | bytes 81952 | tf_op jit(solution)/shard_map/ppermute | solution.py:21
  32.0 1.4 collective-permute-done.3
  33.5 0.0 copy-start.2
  33.5 1.7 %collective-permute-start.9 = (bf16[4,2,80,256]{3,2,1,0:T(8,128)(2,1)S(1)}, bf16[4,2,80,256]{3,2,1,0:T(8,128)(2,1)S(1)}, u32[]{:S(2)}, u32[]{:S(2)}) collective-permute-start(bf16[4,2,80,256]{3,2,1,0:T(8,128)(2,1)S(1)} %pad_maximum_fusion.a0), channel_id=1, source_target_pairs={{0,24},{8,16},{16,8},{24,0},{1,25},{9,17},{17,9},{25,1},{2,26},{10... | collective-permute-start | bytes 983048 | tf_op jit(solution)/shard_map/ppermute | solution.py:21
  35.2 1.1 collective-permute-start.8
  36.3 1.4 collective-permute-start.7
  37.7 3.1 %collective-permute-start.12 = (bf16[4,2,80,256]{3,2,1,0:T(8,128)(2,1)S(1)}, bf16[4,2,80,256]{3,2,1,0:T(8,128)(2,1)S(1)}, u32[]{:S(2)}, u32[]{:S(2)}) collective-permute-start(bf16[4,2,80,256]{3,2,1,0:T(8,128)(2,1)S(1)} %pad_maximum_fusion.1.b0), channel_id=1, source_target_pairs={{0,192},{64,128},{128,64},{192,0},{1,193},{65,129},{129,65},{193,1... | collective-permute-start | bytes 983048 | tf_op jit(solution)/shard_map/ppermute | solution.py:21
  40.8 6.0 %collective-permute-done.9.a3 = bf16[4,2,80,256]{3,2,1,0:T(8,128)(2,1)S(1)} collective-permute-done((bf16[4,2,80,256]{3,2,1,0:T(8,128)(2,1)S(1)}, bf16[4,2,80,256]{3,2,1,0:T(8,128)(2,1)S(1)}, u32[]{:S(2)}, u32[]{:S(2)}) %collective-permute-start.9) | collective-permute-done | bytes 327712 | tf_op jit(solution)/shard_map/ppermute | solution.py:21
  46.7 0.7 collective-permute-start.10
  47.4 0.1 pad_add_fusion.pos
  47.5 1.1 collective-permute-done.7.a1
  48.7 2.9 %collective-permute-done.12.b3 = bf16[4,2,80,256]{3,2,1,0:T(8,128)(2,1)S(1)} collective-permute-done((bf16[4,2,80,256]{3,2,1,0:T(8,128)(2,1)S(1)}, bf16[4,2,80,256]{3,2,1,0:T(8,128)(2,1)S(1)}, u32[]{:S(2)}, u32[]{:S(2)}) %collective-permute-start.12) | collective-permute-done | bytes 327712 | tf_op jit(solution)/shard_map/ppermute | solution.py:21
  51.5 2.4 %collective-permute-done.10.b1 = bf16[4,2,80,256]{3,2,1,0:T(8,128)(2,1)S(1)} collective-permute-done((bf16[4,2,80,256]{3,2,1,0:T(8,128)(2,1)S(1)}, bf16[4,2,80,256]{3,2,1,0:T(8,128)(2,1)S(1)}, u32[]{:S(2)}, u32[]{:S(2)}) %collective-permute-start.10) | collective-permute-done | bytes 327712 | tf_op jit(solution)/shard_map/ppermute | solution.py:21
  53.9 10.8 %logits.1 = (f32[1187,256]{1,0:T(8,128)S(1)}, f32[3,256]{1,0:T(4,128)S(1)}, bf16[2560,256]{1,0:T(8,128)(2,1)}, bf16[2560,256]{1,0:T(8,128)(2,1)}) custom-call(s32[4]{0:T(128)S(1)} %pad_add_fusion.pos, bf16[1187,2560]{1,0:T(8,128)(2,1)} %own_far.3, bf16[1187,2560]{1,0:T(8,128)(2,1)} %copy-done.2, s32[1,256]{1,0:T(1,128)S(1)} %bitcast.85, ...), custom_call_target="tpu_custom_call" | custom-call | tf_op jit(solution)/shard_map/logits/pallas_call | solution.py:145
  64.7 0.0 copy-start.1
  64.7 20.2 %all_to_all.16 = f32[64,3,256]{2,1,0:T(4,128)S(1)} all-to-all(f32[64,3,256]{2,1,0:T(4,128)S(1)} %broadcast_in_dim.11), channel_id=1, replica_groups=mesh['x'=4,'zh'=2,'y'=4,'t'=4,'dp'=2] {'x','y','t'}, dimensions={0} | all-to-all | bytes 393216 | tf_op jit(solution)/shard_map/all_to_all | solution.py:36
  84.9 0.2 slice_reduce_fusion.1
  85.1 2.7 %collective-permute-start.13 = (f32[3,256]{1,0:T(4,128)S(1)}, f32[3,256]{1,0:T(4,128)S(1)}, u32[]{:S(2)}, u32[]{:S(2)}) collective-permute-start(f32[3,256]{1,0:T(4,128)S(1)} %pad_maximum_fusion.3), channel_id=1, source_target_pairs={{0,32},{32,0},{1,33},{33,1},{2,34},{34,2},{3,35},{35,3},{4,36},{36... | collective-permute-start | bytes 9224 | tf_op jit(solution)/shard_map/ppermute | solution.py:163
  87.9 4.9 %collective-permute-done.13 = f32[3,256]{1,0:T(4,128)S(1)} collective-permute-done((f32[3,256]{1,0:T(4,128)S(1)}, f32[3,256]{1,0:T(4,128)S(1)}, u32[]{:S(2)}, u32[]{:S(2)}) %collective-permute-start.13) | collective-permute-done | bytes 3104 | tf_op jit(solution)/shard_map/ppermute | solution.py:163
  92.8 6.7 %grads.1 = (bf16[1187,256]{1,0:T(8,128)(2,1)S(1)}, bf16[4,2,80,256]{3,2,1,0:T(8,128)(2,1)S(1)}, bf16[4,2,80,256]{3,2,1,0:T(8,128)(2,1)S(1)}, bf16[4,2,80,256]{3,...) custom-call(s32[4]{0:T(128)S(1)} %pad_add_fusion.pos, ...), custom_call_target="tpu_custom_call" | custom-call | tf_op jit(solution)/shard_map/grads/pallas_call | solution.py:166
  99.6 0.8 collective-permute-start.14
  100.4 1.3 collective-permute-start.15
  101.6 2.1 %collective-permute-start.16 = (bf16[4,2,80,256]{3,2,1,0:T(8,128)(2,1)S(1)}, bf16[4,2,80,256]{3,2,1,0:T(8,128)(2,1)S(1)}, u32[]{:S(2)}, u32[]{:S(2)}) collective-permute-start(bf16[4,2,80,256]{3,2,1,0:T(8,128)(2,1)S(1)} %get-tuple-element.36), channel_id=1, source_target_pairs={{0,24},{8,16},{16,8},{24,0},{1,25},{9,17},{17,9},{25,1},{2,26},{10... | collective-permute-start | bytes 983048 | tf_op jit(solution)/shard_map/ppermute | solution.py:27
  103.8 0.6 collective-permute-start.17
  104.4 1.0 collective-permute-start.18
  105.4 4.3 %collective-permute-done.14 = bf16[4,2,80,256]{3,2,1,0:T(8,128)(2,1)S(1)} collective-permute-done((bf16[4,2,80,256]{3,2,1,0:T(8,128)(2,1)S(1)}, bf16[4,2,80,256]{3,2,1,0:T(8,128)(2,1)S(1)}, u32[]{:S(2)}, u32[]{:S(2)}) %collective-permute-start.14) | collective-permute-done | bytes 327712 | tf_op jit(solution)/shard_map/ppermute | solution.py:27
  109.7 0.9 collective-permute-start.19
  110.5 0.6 add_subtract_fusion
  111.1 0.3 collective-permute-done.15
  111.4 1.6 %collective-permute-done.16 = bf16[4,2,80,256]{3,2,1,0:T(8,128)(2,1)S(1)} collective-permute-done((bf16[4,2,80,256]{3,2,1,0:T(8,128)(2,1)S(1)}, bf16[4,2,80,256]{3,2,1,0:T(8,128)(2,1)S(1)}, u32[]{:S(2)}, u32[]{:S(2)}) %collective-permute-start.16) | collective-permute-done | bytes 327712 | tf_op jit(solution)/shard_map/ppermute | solution.py:27
  113.0 0.2 add_convert_fusion.1
  113.2 1.3 collective-permute-done.18
  114.5 4.6 %collective-permute-done.19 = bf16[4,2,80,256]{3,2,1,0:T(8,128)(2,1)S(1)} collective-permute-done((bf16[4,2,80,256]{3,2,1,0:T(8,128)(2,1)S(1)}, bf16[4,2,80,256]{3,2,1,0:T(8,128)(2,1)S(1)}, u32[]{:S(2)}, u32[]{:S(2)}) %collective-permute-start.19) | collective-permute-done | bytes 327712 | tf_op jit(solution)/shard_map/ppermute | solution.py:27
  119.2 0.2 add_convert_fusion
  119.4 0.1 collective-permute-start.20
  119.5 0.6 collective-permute-start.22
  120.1 2.8 %collective-permute-start.21 = (bf16[2,80,256]{2,1,0:T(8,128)(2,1)S(1)}, bf16[2,80,256]{2,1,0:T(8,128)(2,1)S(1)}, u32[]{:S(2)}, u32[]{:S(2)}) collective-permute-start(bf16[2,80,256]{2,1,0:T(8,128)(2,1)S(1)} %get-tuple-element.55), channel_id=1, source_target_pairs={{0,64},{64,0},{128,192},{192,128},{1,65},{65,1},{129,193},{193,129... | collective-permute-start | bytes 245768 | tf_op jit(solution)/shard_map/ppermute | solution.py:27
  122.9 0.0 collective-permute-start.26
  123.0 2.5 %collective-permute-done.20 = bf16[2,80,256]{2,1,0:T(8,128)(2,1)S(1)} collective-permute-done((bf16[2,80,256]{2,1,0:T(8,128)(2,1)S(1)}, bf16[2,80,256]{2,1,0:T(8,128)(2,1)S(1)}, u32[]{:S(2)}, u32[]{:S(2)}) %collective-permute-start.20) | collective-permute-done | bytes 81952 | tf_op jit(solution)/shard_map/ppermute | solution.py:27
  125.5 0.6 collective-permute-done.22
  126.1 2.5 %collective-permute-start.25 = (bf16[2,80,256]{2,1,0:T(8,128)(2,1)S(1)}, bf16[2,80,256]{2,1,0:T(8,128)(2,1)S(1)}, u32[]{:S(2)}, u32[]{:S(2)}) collective-permute-start(bf16[2,80,256]{2,1,0:T(8,128)(2,1)S(1)} %get-tuple-element.57), channel_id=1, source_target_pairs={{0,24},{8,16},{16,8},{24,0},{1,25},{9,17},{17,9},{25,1},{2,26},{10... | collective-permute-start | bytes 245768 | tf_op jit(solution)/shard_map/ppermute | solution.py:27
  128.6 1.6 %collective-permute-start.24 = (bf16[2,80,256]{2,1,0:T(8,128)(2,1)S(1)}, bf16[2,80,256]{2,1,0:T(8,128)(2,1)S(1)}, u32[]{:S(2)}, u32[]{:S(2)}) collective-permute-start(bf16[2,80,256]{2,1,0:T(8,128)(2,1)S(1)} %get-tuple-element.58), channel_id=1, source_target_pairs={{0,8},{8,0},{16,24},{24,16},{1,9},{9,1},{17,25},{25,17},{2,10},{10... | collective-permute-start | bytes 245768 | tf_op jit(solution)/shard_map/ppermute | solution.py:27
  130.2 1.3 collective-permute-done.23
  131.6 0.4 collective-permute-done.25
  131.9 1.1 collective-permute-done.24
  133.1 0.8 pad_maximum_fusion.2
  133.9 4.4 %all-to-all-start.2 = ((f32[8,40,256]{2,1,0:T(8,128)}), f32[8,40,256]{2,1,0:T(8,128)S(1)}, u32[]{:S(2)}, u32[]{:S(2)}) async-start(f32[8,40,256]{2,1,0:T(8,128)} %bitcast.36), calls=%async_computation.2 | async-start | bytes 655360 | tf_op jit(solution)/shard_map/all_to_all | solution.py:193
  138.3 1.8 %fusion.17 = f32[1187,2560]{1,0:T(8,128)S(1)} fusion(bf16[1187,256]{1,0:T(8,128)(2,1)S(1)} %collective-permute-done.26, bf16[2560,256]{1,0:T(8,128)(2,1)S(1)} %collective-permute-done.27), kind=kOutput, calls=%fused_computation.48 | convolution fusion | flops 1555824640 | bytes 14073344 | tf_op jit(solution)/shard_map/dot_general | solution.py:186
  140.1 4.5 %fusion = bf16[1187,2560]{1,0:T(8,128)(2,1)} fusion(f32[1187,2560]{1,0:T(8,128)S(1)} %fusion.17, bf16[1187,256]{1,0:T(8,128)(2,1)S(1)} %get-tuple-element.44, bf16[2560,256]{1,0:T(8,128)(2,1)S(1)} %copy-done.3), kind=kOutput, calls=%fused_computation.1 | convolution fusion | flops 1561902080 | bytes 20150784 | tf_op jit(solution)/shard_map/dot_general | solution.py:186
  144.6 4.8 %all-to-all-done.2 = f32[8,40,256]{2,1,0:T(8,128)S(1)} async-done(((f32[8,40,256]{2,1,0:T(8,128)}), f32[8,40,256]{2,1,0:T(8,128)S(1)}, u32[]{:S(2)}, u32[]{:S(2)}) %all-to-all-start.2) | async-done | bytes 327712 | tf_op jit(solution)/shard_map/all_to_all | solution.py:193
  149.4 0.6 reduce_sum.49
  (36 shorter events, 0.4 us)
Async XLA Ops:
  0.6 53.3 %copy-start = (s32[256]{0:T(256)S(1)}, s32[256]{0:T(256)}, u32[]{:S(2)}) copy-start(s32[256]{0:T(256)} %param.6) | copy-start | bytes 3076
  0.6 32.8 %collective-permute-start.6 = (bf16[1187,2560]{1,0:T(8,128)(2,1)}, bf16[1187,2560]{1,0:T(8,128)(2,1)S(1)}, u32[]{:S(2)}, u32[]{:S(2)}) collective-permute-start(bf16[1187,2560]{1,0:T(8,128)(2,1)} %own_far.3), channel_id=1, source_target_pairs={{0,1},{1,0},{2,3},{3,2},{4,5},{5,4},{6,7},{7,6},{8,9},{9,8},{10,11... | collective-permute-start | bytes 18232328 | tf_op jit(solution)/shard_map/ppermute | solution.py:129
  20.2 5.8 %collective-permute-start.2 = (bf16[2,80,256]{2,1,0:T(8,128)(2,1)S(1)}, bf16[2,80,256]{2,1,0:T(8,128)(2,1)S(1)}, u32[]{:S(2)}, u32[]{:S(2)}) collective-permute-start(bf16[2,80,256]{2,1,0:T(8,128)(2,1)S(1)} %get-tuple-element.63), channel_id=1, source_target_pairs={{0,192},{64,128},{128,64},{192,0},{1,193},{65,129},{129,65},{193,1... | collective-permute-start | bytes 245768 | tf_op jit(solution)/shard_map/ppermute | solution.py:21
  23.0 5.9 %collective-permute-start.1 = (bf16[2,80,256]{2,1,0:T(8,128)(2,1)S(1)}, bf16[2,80,256]{2,1,0:T(8,128)(2,1)S(1)}, u32[]{:S(2)}, u32[]{:S(2)}) collective-permute-start(bf16[2,80,256]{2,1,0:T(8,128)(2,1)S(1)} %get-tuple-element.63), channel_id=1, source_target_pairs={{0,128},{64,192},{128,0},{192,64},{1,129},{65,193},{129,1},{193,65... | collective-permute-start | bytes 245768 | tf_op jit(solution)/shard_map/ppermute | solution.py:21
  23.8 5.8 %collective-permute-start = (bf16[2,80,256]{2,1,0:T(8,128)(2,1)S(1)}, bf16[2,80,256]{2,1,0:T(8,128)(2,1)S(1)}, u32[]{:S(2)}, u32[]{:S(2)}) collective-permute-start(bf16[2,80,256]{2,1,0:T(8,128)(2,1)S(1)} %get-tuple-element.63), channel_id=1, source_target_pairs={{0,64},{64,0},{128,192},{192,128},{1,65},{65,1},{129,193},{193,129... | collective-permute-start | bytes 245768 | tf_op jit(solution)/shard_map/ppermute | solution.py:21
  24.4 5.3 %collective-permute-start.5 = (bf16[2,80,256]{2,1,0:T(8,128)(2,1)S(1)}, bf16[2,80,256]{2,1,0:T(8,128)(2,1)S(1)}, u32[]{:S(2)}, u32[]{:S(2)}) collective-permute-start(bf16[2,80,256]{2,1,0:T(8,128)(2,1)S(1)} %get-tuple-element.64), channel_id=1, source_target_pairs={{0,24},{8,16},{16,8},{24,0},{1,25},{9,17},{17,9},{25,1},{2,26},{10... | collective-permute-start | bytes 245768 | tf_op jit(solution)/shard_map/ppermute | solution.py:21
  26.0 6.0 %collective-permute-start.4 = (bf16[2,80,256]{2,1,0:T(8,128)(2,1)S(1)}, bf16[2,80,256]{2,1,0:T(8,128)(2,1)S(1)}, u32[]{:S(2)}, u32[]{:S(2)}) collective-permute-start(bf16[2,80,256]{2,1,0:T(8,128)(2,1)S(1)} %get-tuple-element.64), channel_id=1, source_target_pairs={{0,16},{8,24},{16,0},{24,8},{1,17},{9,25},{17,1},{25,9},{2,18},{10... | collective-permute-start | bytes 245768 | tf_op jit(solution)/shard_map/ppermute | solution.py:21
  29.0 4.4 %collective-permute-start.3 = (bf16[2,80,256]{2,1,0:T(8,128)(2,1)S(1)}, bf16[2,80,256]{2,1,0:T(8,128)(2,1)S(1)}, u32[]{:S(2)}, u32[]{:S(2)}) collective-permute-start(bf16[2,80,256]{2,1,0:T(8,128)(2,1)S(1)} %get-tuple-element.64), channel_id=1, source_target_pairs={{0,8},{8,0},{16,24},{24,16},{1,9},{9,1},{17,25},{25,17},{2,10},{10... | collective-permute-start | bytes 245768 | tf_op jit(solution)/shard_map/ppermute | solution.py:21
  33.5 13.2 %copy-start.2 = (bf16[1187,2560]{1,0:T(8,128)(2,1)}, bf16[1187,2560]{1,0:T(8,128)(2,1)S(1)}, u32[]{:S(2)}) copy-start(bf16[1187,2560]{1,0:T(8,128)(2,1)S(1)} %collective-permute-done.6.other_far) | copy-start | bytes 18232324
  33.5 13.2 %collective-permute-start.9 = (bf16[4,2,80,256]{3,2,1,0:T(8,128)(2,1)S(1)}, bf16[4,2,80,256]{3,2,1,0:T(8,128)(2,1)S(1)}, u32[]{:S(2)}, u32[]{:S(2)}) collective-permute-start(bf16[4,2,80,256]{3,2,1,0:T(8,128)(2,1)S(1)} %pad_maximum_fusion.a0), channel_id=1, source_target_pairs={{0,24},{8,16},{16,8},{24,0},{1,25},{9,17},{17,9},{25,1},{2,26},{10... | collective-permute-start | bytes 983048 | tf_op jit(solution)/shard_map/ppermute | solution.py:21
  35.2 12.4 %collective-permute-start.8 = (bf16[4,2,80,256]{3,2,1,0:T(8,128)(2,1)S(1)}, bf16[4,2,80,256]{3,2,1,0:T(8,128)(2,1)S(1)}, u32[]{:S(2)}, u32[]{:S(2)}) collective-permute-start(bf16[4,2,80,256]{3,2,1,0:T(8,128)(2,1)S(1)} %pad_maximum_fusion.a0), channel_id=1, source_target_pairs={{0,16},{8,24},{16,0},{24,8},{1,17},{9,25},{17,1},{25,9},{2,18},{10... | collective-permute-start | bytes 983048 | tf_op jit(solution)/shard_map/ppermute | solution.py:21
  36.3 12.4 %collective-permute-start.7 = (bf16[4,2,80,256]{3,2,1,0:T(8,128)(2,1)S(1)}, bf16[4,2,80,256]{3,2,1,0:T(8,128)(2,1)S(1)}, u32[]{:S(2)}, u32[]{:S(2)}) collective-permute-start(bf16[4,2,80,256]{3,2,1,0:T(8,128)(2,1)S(1)} %pad_maximum_fusion.a0), channel_id=1, source_target_pairs={{0,8},{8,0},{16,24},{24,16},{1,9},{9,1},{17,25},{25,17},{2,10},{10... | collective-permute-start | bytes 983048 | tf_op jit(solution)/shard_map/ppermute | solution.py:21
  37.7 13.8 %collective-permute-start.12 = (bf16[4,2,80,256]{3,2,1,0:T(8,128)(2,1)S(1)}, bf16[4,2,80,256]{3,2,1,0:T(8,128)(2,1)S(1)}, u32[]{:S(2)}, u32[]{:S(2)}) collective-permute-start(bf16[4,2,80,256]{3,2,1,0:T(8,128)(2,1)S(1)} %pad_maximum_fusion.1.b0), channel_id=1, source_target_pairs={{0,192},{64,128},{128,64},{192,0},{1,193},{65,129},{129,65},{193,1... | collective-permute-start | bytes 983048 | tf_op jit(solution)/shard_map/ppermute | solution.py:21
  40.8 10.8 %collective-permute-start.11 = (bf16[4,2,80,256]{3,2,1,0:T(8,128)(2,1)S(1)}, bf16[4,2,80,256]{3,2,1,0:T(8,128)(2,1)S(1)}, u32[]{:S(2)}, u32[]{:S(2)}) collective-permute-start(bf16[4,2,80,256]{3,2,1,0:T(8,128)(2,1)S(1)} %pad_maximum_fusion.1.b0), channel_id=1, source_target_pairs={{0,128},{64,192},{128,0},{192,64},{1,129},{65,193},{129,1},{193,65... | collective-permute-start | bytes 983048 | tf_op jit(solution)/shard_map/ppermute | solution.py:21
  46.7 7.2 %collective-permute-start.10 = (bf16[4,2,80,256]{3,2,1,0:T(8,128)(2,1)S(1)}, bf16[4,2,80,256]{3,2,1,0:T(8,128)(2,1)S(1)}, u32[]{:S(2)}, u32[]{:S(2)}) collective-permute-start(bf16[4,2,80,256]{3,2,1,0:T(8,128)(2,1)S(1)} %pad_maximum_fusion.1.b0), channel_id=1, source_target_pairs={{0,64},{64,0},{128,192},{192,128},{1,65},{65,1},{129,193},{193,129... | collective-permute-start | bytes 983048 | tf_op jit(solution)/shard_map/ppermute | solution.py:21
  53.9 38.9 %slice-start = ((s8[6103040]{0:T(1024)(128)(4,1)}), s8[4194304]{0:T(1024)(128)(4,1)S(1)}, s32[]{:S(2)}) async-start(s8[6103040]{0:T(1024)(128)(4,1)} %bitcast.83), calls=%async_computation.3 | async-start | bytes 8388608
  53.9 38.9 %slice-start.1 = ((s8[6103040]{0:T(1024)(128)(4,1)}), s8[1908736]{0:T(1024)(128)(4,1)S(1)}, s32[]{:S(2)}) async-start(s8[6103040]{0:T(1024)(128)(4,1)} %bitcast.83), calls=%async_computation.4 | async-start | bytes 3817472
  64.7 28.1 %copy-start.1 = (f32[256]{0:T(256)S(1)}, f32[256]{0:T(256)}, u32[]{:S(2)}) copy-start(f32[256]{0:T(256)} %param.7) | copy-start | bytes 3076
  85.1 7.6 %collective-permute-start.13 = (f32[3,256]{1,0:T(4,128)S(1)}, f32[3,256]{1,0:T(4,128)S(1)}, u32[]{:S(2)}, u32[]{:S(2)}) collective-permute-start(f32[3,256]{1,0:T(4,128)S(1)} %pad_maximum_fusion.3), channel_id=1, source_target_pairs={{0,32},{32,0},{1,33},{33,1},{2,34},{34,2},{3,35},{35,3},{4,36},{36... | collective-permute-start | bytes 9224 | tf_op jit(solution)/shard_map/ppermute | solution.py:163
  99.6 10.1 %collective-permute-start.14 = (bf16[4,2,80,256]{3,2,1,0:T(8,128)(2,1)S(1)}, bf16[4,2,80,256]{3,2,1,0:T(8,128)(2,1)S(1)}, u32[]{:S(2)}, u32[]{:S(2)}) collective-permute-start(bf16[4,2,80,256]{3,2,1,0:T(8,128)(2,1)S(1)} %get-tuple-element.34), channel_id=1, source_target_pairs={{0,16},{8,24},{16,0},{24,8},{1,17},{9,25},{17,1},{25,9},{2,18},{10... | collective-permute-start | bytes 983048 | tf_op jit(solution)/shard_map/ppermute | solution.py:27
  100.4 11.1 %collective-permute-start.15 = (bf16[4,2,80,256]{3,2,1,0:T(8,128)(2,1)S(1)}, bf16[4,2,80,256]{3,2,1,0:T(8,128)(2,1)S(1)}, u32[]{:S(2)}, u32[]{:S(2)}) collective-permute-start(bf16[4,2,80,256]{3,2,1,0:T(8,128)(2,1)S(1)} %get-tuple-element.35), channel_id=1, source_target_pairs={{0,8},{8,0},{16,24},{24,16},{1,9},{9,1},{17,25},{25,17},{2,10},{10... | collective-permute-start | bytes 983048 | tf_op jit(solution)/shard_map/ppermute | solution.py:27
  101.6 11.4 %collective-permute-start.16 = (bf16[4,2,80,256]{3,2,1,0:T(8,128)(2,1)S(1)}, bf16[4,2,80,256]{3,2,1,0:T(8,128)(2,1)S(1)}, u32[]{:S(2)}, u32[]{:S(2)}) collective-permute-start(bf16[4,2,80,256]{3,2,1,0:T(8,128)(2,1)S(1)} %get-tuple-element.36), channel_id=1, source_target_pairs={{0,24},{8,16},{16,8},{24,0},{1,25},{9,17},{17,9},{25,1},{2,26},{10... | collective-permute-start | bytes 983048 | tf_op jit(solution)/shard_map/ppermute | solution.py:27
  103.8 9.4 %collective-permute-start.17 = (bf16[4,2,80,256]{3,2,1,0:T(8,128)(2,1)S(1)}, bf16[4,2,80,256]{3,2,1,0:T(8,128)(2,1)S(1)}, u32[]{:S(2)}, u32[]{:S(2)}) collective-permute-start(bf16[4,2,80,256]{3,2,1,0:T(8,128)(2,1)S(1)} %get-tuple-element.38), channel_id=1, source_target_pairs={{0,128},{64,192},{128,0},{192,64},{1,129},{65,193},{129,1},{193,65... | collective-permute-start | bytes 983048 | tf_op jit(solution)/shard_map/ppermute | solution.py:27
  104.4 10.1 %collective-permute-start.18 = (bf16[4,2,80,256]{3,2,1,0:T(8,128)(2,1)S(1)}, bf16[4,2,80,256]{3,2,1,0:T(8,128)(2,1)S(1)}, u32[]{:S(2)}, u32[]{:S(2)}) collective-permute-start(bf16[4,2,80,256]{3,2,1,0:T(8,128)(2,1)S(1)} %get-tuple-element.39), channel_id=1, source_target_pairs={{0,64},{64,0},{128,192},{192,128},{1,65},{65,1},{129,193},{193,129... | collective-permute-start | bytes 983048 | tf_op jit(solution)/shard_map/ppermute | solution.py:27
  109.7 9.5 %collective-permute-start.19 = (bf16[4,2,80,256]{3,2,1,0:T(8,128)(2,1)S(1)}, bf16[4,2,80,256]{3,2,1,0:T(8,128)(2,1)S(1)}, u32[]{:S(2)}, u32[]{:S(2)}) collective-permute-start(bf16[4,2,80,256]{3,2,1,0:T(8,128)(2,1)S(1)} %get-tuple-element.40), channel_id=1, source_target_pairs={{0,192},{64,128},{128,64},{192,0},{1,193},{65,129},{129,65},{193,1... | collective-permute-start | bytes 983048 | tf_op jit(solution)/shard_map/ppermute | solution.py:27
  111.4 26.8 %collective-permute-start.27 = (bf16[2560,256]{1,0:T(8,128)(2,1)}, bf16[2560,256]{1,0:T(8,128)(2,1)S(1)}, u32[]{:S(2)}, u32[]{:S(2)}) collective-permute-start(bf16[2560,256]{1,0:T(8,128)(2,1)} %get-tuple-element.46), channel_id=1, source_target_pairs={{0,1},{1,0},{2,3},{3,2},{4,5},{5,4},{6,7},{7,6},{8,9},{9,8},{10,11... | collective-permute-start | bytes 3932168 | tf_op jit(solution)/shard_map/ppermute | solution.py:162
  119.4 6.1 %collective-permute-start.20 = (bf16[2,80,256]{2,1,0:T(8,128)(2,1)S(1)}, bf16[2,80,256]{2,1,0:T(8,128)(2,1)S(1)}, u32[]{:S(2)}, u32[]{:S(2)}) collective-permute-start(bf16[2,80,256]{2,1,0:T(8,128)(2,1)S(1)} %get-tuple-element.53), channel_id=1, source_target_pairs={{0,128},{64,192},{128,0},{192,64},{1,129},{65,193},{129,1},{193,65... | collective-permute-start | bytes 245768 | tf_op jit(solution)/shard_map/ppermute | solution.py:27
  119.5 6.6 %collective-permute-start.22 = (bf16[2,80,256]{2,1,0:T(8,128)(2,1)S(1)}, bf16[2,80,256]{2,1,0:T(8,128)(2,1)S(1)}, u32[]{:S(2)}, u32[]{:S(2)}) collective-permute-start(bf16[2,80,256]{2,1,0:T(8,128)(2,1)S(1)} %get-tuple-element.54), channel_id=1, source_target_pairs={{0,192},{64,128},{128,64},{192,0},{1,193},{65,129},{129,65},{193,1... | collective-permute-start | bytes 245768 | tf_op jit(solution)/shard_map/ppermute | solution.py:27
  120.1 8.5 %collective-permute-start.21 = (bf16[2,80,256]{2,1,0:T(8,128)(2,1)S(1)}, bf16[2,80,256]{2,1,0:T(8,128)(2,1)S(1)}, u32[]{:S(2)}, u32[]{:S(2)}) collective-permute-start(bf16[2,80,256]{2,1,0:T(8,128)(2,1)S(1)} %get-tuple-element.55), channel_id=1, source_target_pairs={{0,64},{64,0},{128,192},{192,128},{1,65},{65,1},{129,193},{193,129... | collective-permute-start | bytes 245768 | tf_op jit(solution)/shard_map/ppermute | solution.py:27
  122.9 15.3 %collective-permute-start.26 = (bf16[1187,256]{1,0:T(8,128)(2,1)S(1)}, bf16[1187,256]{1,0:T(8,128)(2,1)S(1)}, u32[]{:S(2)}, u32[]{:S(2)}) collective-permute-start(bf16[1187,256]{1,0:T(8,128)(2,1)S(1)} %get-tuple-element.44), channel_id=1, source_target_pairs={{0,1},{1,0},{2,3},{3,2},{4,5},{5,4},{6,7},{7,6},{8,9},{9,8},{10,11... | collective-permute-start | bytes 1823240 | tf_op jit(solution)/shard_map/ppermute | solution.py:185
  125.5 6.1 %collective-permute-start.23 = (bf16[2,80,256]{2,1,0:T(8,128)(2,1)S(1)}, bf16[2,80,256]{2,1,0:T(8,128)(2,1)S(1)}, u32[]{:S(2)}, u32[]{:S(2)}) collective-permute-start(bf16[2,80,256]{2,1,0:T(8,128)(2,1)S(1)} %get-tuple-element.56), channel_id=1, source_target_pairs={{0,16},{8,24},{16,0},{24,8},{1,17},{9,25},{17,1},{25,9},{2,18},{10... | collective-permute-start | bytes 245768 | tf_op jit(solution)/shard_map/ppermute | solution.py:27
  126.1 5.8 %collective-permute-start.25 = (bf16[2,80,256]{2,1,0:T(8,128)(2,1)S(1)}, bf16[2,80,256]{2,1,0:T(8,128)(2,1)S(1)}, u32[]{:S(2)}, u32[]{:S(2)}) collective-permute-start(bf16[2,80,256]{2,1,0:T(8,128)(2,1)S(1)} %get-tuple-element.57), channel_id=1, source_target_pairs={{0,24},{8,16},{16,8},{24,0},{1,25},{9,17},{17,9},{25,1},{2,26},{10... | collective-permute-start | bytes 245768 | tf_op jit(solution)/shard_map/ppermute | solution.py:27
  128.6 4.4 %collective-permute-start.24 = (bf16[2,80,256]{2,1,0:T(8,128)(2,1)S(1)}, bf16[2,80,256]{2,1,0:T(8,128)(2,1)S(1)}, u32[]{:S(2)}, u32[]{:S(2)}) collective-permute-start(bf16[2,80,256]{2,1,0:T(8,128)(2,1)S(1)} %get-tuple-element.58), channel_id=1, source_target_pairs={{0,8},{8,0},{16,24},{24,16},{1,9},{9,1},{17,25},{25,17},{2,10},{10... | collective-permute-start | bytes 245768 | tf_op jit(solution)/shard_map/ppermute | solution.py:27
  133.9 15.6 %all-to-all-start.2 = ((f32[8,40,256]{2,1,0:T(8,128)}), f32[8,40,256]{2,1,0:T(8,128)S(1)}, u32[]{:S(2)}, u32[]{:S(2)}) async-start(f32[8,40,256]{2,1,0:T(8,128)} %bitcast.36), calls=%async_computation.2 | async-start | bytes 655360 | tf_op jit(solution)/shard_map/all_to_all | solution.py:193
  138.3 1.8 %copy-start.3 = (bf16[2560,256]{1,0:T(8,128)(2,1)S(1)}, bf16[2560,256]{1,0:T(8,128)(2,1)}, u32[]{:S(2)}) copy-start(bf16[2560,256]{1,0:T(8,128)(2,1)} %get-tuple-element.45) | copy-start | bytes 3932164

commit v3 on v2

--- a/solution.py
+++ b/solution.py
@@ -56,8 +56,10 @@
                     row = pl.multiple_of(block * 2 * side + side, 16)
                     act(seconds[kx], (ky, zh), half, pl.ds(row, side))
 
-        pl.when(place < 2)(lambda: visit(own))
-        pl.when(place >= 2)(lambda: visit(other))
+        if own is not None:
+            pl.when(place < 2)(lambda: visit(own))
+        if other is not None:
+            pl.when(place >= 2)(lambda: visit(other))
 
 
 def fetch(own_far, other_far, own, other, sems):
@@ -72,7 +74,8 @@
 
 
 def logits_kernel(pos, own_far, other_far, labels, a0, a1, a2, a3, b0, b1, b2, b3,
-                  logits, stats, feats_own, feats_other, own, other, sems):
+                  logits, stats, own_out, other_out, own, other, sems,
+                  feats_own, feats_other, out_sems):
     copies = fetch(own_far, other_far, own, other, sems)
 
     def place(piece, index, half, rows):
@@ -80,6 +83,12 @@
 
     firsts, seconds = (a0, a1, a2, a3), (b0, b1, b2, b3)
     each_piece(pos, a0.shape[2], firsts, seconds, feats_own, feats_other, place)
+    leaving = [
+        pltpu.make_async_copy(feats_own, own_out, out_sems.at[0]),
+        pltpu.make_async_copy(feats_other, other_out, out_sems.at[1]),
+    ]
+    for copy in leaving:
+        copy.start()
     copies[0].wait()
     copies[1].wait()
     logits[...] = jnp.dot(own[...], feats_own[...], preferred_element_type=F32)
@@ -94,6 +103,8 @@
     stats[0:1, :] = peak
     stats[1:2, :] = jnp.sum(jnp.exp(value - peak), axis=0, keepdims=True)
     stats[2:3, :] = jnp.sum(jnp.where(rows == labels[...], value, 0.0), axis=0, keepdims=True)
+    for copy in leaving:
+        copy.wait()
 
 
 def grad_kernel(pos, own_far, other_far, logits, labels, loss_weight, stats,
@@ -107,18 +118,20 @@
     grad[...] = result.astype(BF)
     grad_t[...] = result.T.astype(BF)
     width = own.shape[1] // 2
+    firsts, seconds = (a0, a1, a2, a3), (b0, b1, b2, b3)
+
+    def take(piece, index, half, rows):
+        piece[index] = half[rows, :]
+
     for j in range(4):
         copies[j].wait()
         weight, part = (own, part_own) if j < 2 else (other, part_other)
         span = slice((j % 2) * width, (j % 2 + 1) * width)
         piece = jnp.dot(grad_t[...], weight[:, span], preferred_element_type=F32)
         part[span, :] = piece.T.astype(BF)
-
-    def take(piece, index, half, rows):
-        piece[index] = half[rows, :]
-
-    firsts, seconds = (a0, a1, a2, a3), (b0, b1, b2, b3)
-    each_piece(pos, a0.shape[2], firsts, seconds, part_own, part_other, take)
+        if j == 1:
+            each_piece(pos, a0.shape[2], firsts, seconds, part_own, None, take)
+    each_piece(pos, a0.shape[2], firsts, seconds, None, part_other, take)
 
 
 def per_device(hidden, head_weight, labels, loss_weight):
@@ -145,14 +158,16 @@
     logits, stats, feats_own, feats_other = pl.pallas_call(
         logits_kernel,
         in_specs=[SMEM] + [HBM] * 2 + [VMEM] * 9,
-        out_specs=[VMEM] * 4,
+        out_specs=[VMEM] * 2 + [HBM] * 2,
         out_shape=[
             jax.ShapeDtypeStruct((rows, tokens), F32),
             jax.ShapeDtypeStruct((3, tokens), F32),
             jax.ShapeDtypeStruct((half, tokens), BF),
             jax.ShapeDtypeStruct((half, tokens), BF),
         ],
-        scratch_shapes=weights,
+        scratch_shapes=weights
+        + [pltpu.VMEM((half, tokens), BF)] * 2
+        + [pltpu.SemaphoreType.DMA((2,))],
         compiler_params=pltpu.CompilerParams(vmem_limit_bytes=50 * 1024 * 1024),
         name="logits",
     )(pos, head_weight, weight_other, labels, *first, *second)

time: 150 us -> 151 us (level)
  no operation moved by 1% of the time
where the time goes in v3:
time: 151 us
  waiting for transfers between devices  44.7 us (30%)
  blocking collectives  38.9 us (26%)
  starting transfers between devices  38.2 us (25%)
  Pallas kernels  18.5 us (12%)
  matrix products  6.32 us (4%)
  other arithmetic  2.86 us (2%)
    all_to_all x2, blocking collectives, share(): lax.all_to_all(jnp.broadcast_to(block[None], (n,) + block.shape), axes, 0...  38.9 us
    ppermute x12, waiting for transfers between devices, collect(): got = [lax.ppermute(blocks[k], axis, paired(4, k)) for k in (2, 1, 3)]  18.1 us
    ppermute x12, waiting for transfers between devices, spread(): got = {k: lax.ppermute(block, axis, paired(4, k)) for k in (2, 1, 3)}  16.9 us
    ppermute x12, starting transfers between devices, spread(): got = {k: lax.ppermute(block, axis, paired(4, k)) for k in (2, 1, 3)}  16.6 us
    ppermute x12, starting transfers between devices, collect(): got = [lax.ppermute(blocks[k], axis, paired(4, k)) for k in (2, 1, 3)]  14.3 us
    pallas_call x1, Pallas kernels, per_device(): pl.pallas_call(logits_kernel, in_specs=[SMEM] + [HBM] * 2 + [VMEM] * 9, o...  11.7 us
    pallas_call x1, Pallas kernels, per_device(): pl.pallas_call(grad_kernel, in_specs=[SMEM] + [HBM] * 2 + [VMEM] * 4, out...  6.73 us
    dot_general x2, matrix products, per_device(): lax.dot_general(a, b, (((1,), (1,)), ((), ())), preferred_element_type=F32)  6.32 us
  transfers between devices with their start and end apart: 29, of which 20 were waited for; matrix products, arithmetic and copies ran while one was open for 6% of the time, Pallas kernels for 0%

profile of v3, /device:TPU:8, one launch (start us, length us, event | category | flops | bytes accessed | tf_op | source)
XLA Modules:
  0.0 151.0 jit_solution(10787038775359080454)
XLA Ops:
  0.6 0.1 collective-permute-start.6
  0.7 0.7 broadcast_in_dim.8
  1.5 18.7 %all_to_all.15 = bf16[8,40,256]{2,1,0:T(8,128)(2,1)S(1)} all-to-all(bf16[8,40,256]{2,1,0:T(8,128)(2,1)S(1)} %broadcast_in_dim.8), channel_id=1, replica_groups=mesh['x'=4,'zh'=2,'y'=4,'t'=4,'dp'=2] {'zh','t'}, dimensions={0} | all-to-all | bytes 327680 | tf_op jit(solution)/shard_map/all_to_all | solution.py:36
  20.2 2.8 %collective-permute-start.2 = (bf16[2,80,256]{2,1,0:T(8,128)(2,1)S(1)}, bf16[2,80,256]{2,1,0:T(8,128)(2,1)S(1)}, u32[]{:S(2)}, u32[]{:S(2)}) collective-permute-start(bf16[2,80,256]{2,1,0:T(8,128)(2,1)S(1)} %get-tuple-element.63), channel_id=1, source_target_pairs={{0,192},{64,128},{128,64},{192,0},{1,193},{65,129},{129,65},{193,1... | collective-permute-start | bytes 245768 | tf_op jit(solution)/shard_map/ppermute | solution.py:21
  23.0 0.8 collective-permute-start.1
  23.8 0.5 collective-permute-start
  24.4 1.6 %collective-permute-start.5 = (bf16[2,80,256]{2,1,0:T(8,128)(2,1)S(1)}, bf16[2,80,256]{2,1,0:T(8,128)(2,1)S(1)}, u32[]{:S(2)}, u32[]{:S(2)}) collective-permute-start(bf16[2,80,256]{2,1,0:T(8,128)(2,1)S(1)} %get-tuple-element.64), channel_id=1, source_target_pairs={{0,24},{8,16},{16,8},{24,0},{1,25},{9,17},{17,9},{25,1},{2,26},{10... | collective-permute-start | bytes 245768 | tf_op jit(solution)/shard_map/ppermute | solution.py:21
  26.0 0.0 collective-permute-done.2
  26.0 2.3 %collective-permute-start.4 = (bf16[2,80,256]{2,1,0:T(8,128)(2,1)S(1)}, bf16[2,80,256]{2,1,0:T(8,128)(2,1)S(1)}, u32[]{:S(2)}, u32[]{:S(2)}) collective-permute-start(bf16[2,80,256]{2,1,0:T(8,128)(2,1)S(1)} %get-tuple-element.64), channel_id=1, source_target_pairs={{0,16},{8,24},{16,0},{24,8},{1,17},{9,25},{17,1},{25,9},{2,18},{10... | collective-permute-start | bytes 245768 | tf_op jit(solution)/shard_map/ppermute | solution.py:21
  28.2 0.7 collective-permute-done.1
  29.0 0.6 collective-permute-start.3
  29.6 0.0 collective-permute-done
  29.7 0.1 collective-permute-done.5
  29.7 2.3 %collective-permute-done.4 = bf16[2,80,256]{2,1,0:T(8,128)(2,1)S(1)} collective-permute-done((bf16[2,80,256]{2,1,0:T(8,128)(2,1)S(1)}, bf16[2,80,256]{2,1,0:T(8,128)(2,1)S(1)}, u32[]{:S(2)}, u32[]{:S(2)}) %collective-permute-start.4) | collective-permute-done | bytes 81952 | tf_op jit(solution)/shard_map/ppermute | solution.py:21
  32.0 1.4 collective-permute-done.3
  33.5 0.0 copy-start.2
  33.5 1.7 %collective-permute-start.9 = (bf16[4,2,80,256]{3,2,1,0:T(8,128)(2,1)S(1)}, bf16[4,2,80,256]{3,2,1,0:T(8,128)(2,1)S(1)}, u32[]{:S(2)}, u32[]{:S(2)}) collective-permute-start(bf16[4,2,80,256]{3,2,1,0:T(8,128)(2,1)S(1)} %pad_maximum_fusion.a0), channel_id=1, source_target_pairs={{0,24},{8,16},{16,8},{24,0},{1,25},{9,17},{17,9},{25,1},{2,26},{10... | collective-permute-start | bytes 983048 | tf_op jit(solution)/shard_map/ppermute | solution.py:21
  35.2 1.1 collective-permute-start.8
  36.3 1.4 collective-permute-start.7
  37.7 3.1 %collective-permute-start.12 = (bf16[4,2,80,256]{3,2,1,0:T(8,128)(2,1)S(1)}, bf16[4,2,80,256]{3,2,1,0:T(8,128)(2,1)S(1)}, u32[]{:S(2)}, u32[]{:S(2)}) collective-permute-start(bf16[4,2,80,256]{3,2,1,0:T(8,128)(2,1)S(1)} %pad_maximum_fusion.1.b0), channel_id=1, source_target_pairs={{0,192},{64,128},{128,64},{192,0},{1,193},{65,129},{129,65},{193,1... | collective-permute-start | bytes 983048 | tf_op jit(solution)/shard_map/ppermute | solution.py:21
  40.8 6.0 %collective-permute-done.9.a3 = bf16[4,2,80,256]{3,2,1,0:T(8,128)(2,1)S(1)} collective-permute-done((bf16[4,2,80,256]{3,2,1,0:T(8,128)(2,1)S(1)}, bf16[4,2,80,256]{3,2,1,0:T(8,128)(2,1)S(1)}, u32[]{:S(2)}, u32[]{:S(2)}) %collective-permute-start.9) | collective-permute-done | bytes 327712 | tf_op jit(solution)/shard_map/ppermute | solution.py:21
  46.7 0.7 collective-permute-start.10
  47.4 0.1 pad_add_fusion.pos
  47.5 1.1 collective-permute-done.7.a1
  48.7 2.9 %collective-permute-done.12.b3 = bf16[4,2,80,256]{3,2,1,0:T(8,128)(2,1)S(1)} collective-permute-done((bf16[4,2,80,256]{3,2,1,0:T(8,128)(2,1)S(1)}, bf16[4,2,80,256]{3,2,1,0:T(8,128)(2,1)S(1)}, u32[]{:S(2)}, u32[]{:S(2)}) %collective-permute-start.12) | collective-permute-done | bytes 327712 | tf_op jit(solution)/shard_map/ppermute | solution.py:21
  51.5 2.4 %collective-permute-done.10.b1 = bf16[4,2,80,256]{3,2,1,0:T(8,128)(2,1)S(1)} collective-permute-done((bf16[4,2,80,256]{3,2,1,0:T(8,128)(2,1)S(1)}, bf16[4,2,80,256]{3,2,1,0:T(8,128)(2,1)S(1)}, u32[]{:S(2)}, u32[]{:S(2)}) %collective-permute-start.10) | collective-permute-done | bytes 327712 | tf_op jit(solution)/shard_map/ppermute | solution.py:21
  53.9 11.7 %logits.1 = (f32[1187,256]{1,0:T(8,128)S(1)}, f32[3,256]{1,0:T(4,128)S(1)}, bf16[2560,256]{1,0:T(8,128)(2,1)}, bf16[2560,256]{1,0:T(8,128)(2,1)}) custom-call(s32[4]{0:T(128)S(1)} %pad_add_fusion.pos, bf16[1187,2560]{1,0:T(8,128)(2,1)} %own_far.3, bf16[1187,2560]{1,0:T(8,128)(2,1)} %copy-done.2, s32[1,256]{1,0:T(1,128)S(1)} %bitcast.85, ...), custom_call_target="tpu_custom_call" | custom-call | tf_op jit(solution)/shard_map/logits/pallas_call | solution.py:158
  65.6 0.0 copy-start.1
  65.7 20.2 %all_to_all.16 = f32[64,3,256]{2,1,0:T(4,128)S(1)} all-to-all(f32[64,3,256]{2,1,0:T(4,128)S(1)} %broadcast_in_dim.11), channel_id=1, replica_groups=mesh['x'=4,'zh'=2,'y'=4,'t'=4,'dp'=2] {'x','y','t'}, dimensions={0} | all-to-all | bytes 393216 | tf_op jit(solution)/shard_map/all_to_all | solution.py:36
  85.9 0.2 slice_reduce_fusion.1
  86.1 2.7 %collective-permute-start.13 = (f32[3,256]{1,0:T(4,128)S(1)}, f32[3,256]{1,0:T(4,128)S(1)}, u32[]{:S(2)}, u32[]{:S(2)}) collective-permute-start(f32[3,256]{1,0:T(4,128)S(1)} %pad_maximum_fusion.3), channel_id=1, source_target_pairs={{0,32},{32,0},{1,33},{33,1},{2,34},{34,2},{3,35},{35,3},{4,36},{36... | collective-permute-start | bytes 9224 | tf_op jit(solution)/shard_map/ppermute | solution.py:178
  88.8 4.9 %collective-permute-done.13 = f32[3,256]{1,0:T(4,128)S(1)} collective-permute-done((f32[3,256]{1,0:T(4,128)S(1)}, f32[3,256]{1,0:T(4,128)S(1)}, u32[]{:S(2)}, u32[]{:S(2)}) %collective-permute-start.13) | collective-permute-done | bytes 3104 | tf_op jit(solution)/shard_map/ppermute | solution.py:178
  93.8 6.7 %grads.1 = (bf16[1187,256]{1,0:T(8,128)(2,1)S(1)}, bf16[4,2,80,256]{3,2,1,0:T(8,128)(2,1)S(1)}, bf16[4,2,80,256]{3,2,1,0:T(8,128)(2,1)S(1)}, bf16[4,2,80,256]{3,...) custom-call(s32[4]{0:T(128)S(1)} %pad_add_fusion.pos, ...), custom_call_target="tpu_custom_call" | custom-call | tf_op jit(solution)/shard_map/grads/pallas_call | solution.py:181
  100.5 0.8 collective-permute-start.14
  101.3 1.3 collective-permute-start.15
  102.6 2.1 %collective-permute-start.16 = (bf16[4,2,80,256]{3,2,1,0:T(8,128)(2,1)S(1)}, bf16[4,2,80,256]{3,2,1,0:T(8,128)(2,1)S(1)}, u32[]{:S(2)}, u32[]{:S(2)}) collective-permute-start(bf16[4,2,80,256]{3,2,1,0:T(8,128)(2,1)S(1)} %get-tuple-element.36), channel_id=1, source_target_pairs={{0,24},{8,16},{16,8},{24,0},{1,25},{9,17},{17,9},{25,1},{2,26},{10... | collective-permute-start | bytes 983048 | tf_op jit(solution)/shard_map/ppermute | solution.py:27
  104.7 0.6 collective-permute-start.17
  105.3 1.0 collective-permute-start.18
  106.3 4.3 %collective-permute-done.14 = bf16[4,2,80,256]{3,2,1,0:T(8,128)(2,1)S(1)} collective-permute-done((bf16[4,2,80,256]{3,2,1,0:T(8,128)(2,1)S(1)}, bf16[4,2,80,256]{3,2,1,0:T(8,128)(2,1)S(1)}, u32[]{:S(2)}, u32[]{:S(2)}) %collective-permute-start.14) | collective-permute-done | bytes 327712 | tf_op jit(solution)/shard_map/ppermute | solution.py:27
  110.6 0.9 collective-permute-start.19
  111.5 0.6 add_subtract_fusion
  112.1 0.3 collective-permute-done.15
  112.4 1.6 %collective-permute-done.16 = bf16[4,2,80,256]{3,2,1,0:T(8,128)(2,1)S(1)} collective-permute-done((bf16[4,2,80,256]{3,2,1,0:T(8,128)(2,1)S(1)}, bf16[4,2,80,256]{3,2,1,0:T(8,128)(2,1)S(1)}, u32[]{:S(2)}, u32[]{:S(2)}) %collective-permute-start.16) | collective-permute-done | bytes 327712 | tf_op jit(solution)/shard_map/ppermute | solution.py:27
  114.0 0.2 add_convert_fusion.1
  114.2 1.3 collective-permute-done.18
  115.5 4.6 %collective-permute-done.19 = bf16[4,2,80,256]{3,2,1,0:T(8,128)(2,1)S(1)} collective-permute-done((bf16[4,2,80,256]{3,2,1,0:T(8,128)(2,1)S(1)}, bf16[4,2,80,256]{3,2,1,0:T(8,128)(2,1)S(1)}, u32[]{:S(2)}, u32[]{:S(2)}) %collective-permute-start.19) | collective-permute-done | bytes 327712 | tf_op jit(solution)/shard_map/ppermute | solution.py:27
  120.1 0.2 add_convert_fusion
  120.3 0.1 collective-permute-start.20
  120.4 0.6 collective-permute-start.22
  121.0 2.8 %collective-permute-start.21 = (bf16[2,80,256]{2,1,0:T(8,128)(2,1)S(1)}, bf16[2,80,256]{2,1,0:T(8,128)(2,1)S(1)}, u32[]{:S(2)}, u32[]{:S(2)}) collective-permute-start(bf16[2,80,256]{2,1,0:T(8,128)(2,1)S(1)} %get-tuple-element.55), channel_id=1, source_target_pairs={{0,64},{64,0},{128,192},{192,128},{1,65},{65,1},{129,193},{193,129... | collective-permute-start | bytes 245768 | tf_op jit(solution)/shard_map/ppermute | solution.py:27
  123.9 0.0 collective-permute-start.26
  123.9 2.5 %collective-permute-done.20 = bf16[2,80,256]{2,1,0:T(8,128)(2,1)S(1)} collective-permute-done((bf16[2,80,256]{2,1,0:T(8,128)(2,1)S(1)}, bf16[2,80,256]{2,1,0:T(8,128)(2,1)S(1)}, u32[]{:S(2)}, u32[]{:S(2)}) %collective-permute-start.20) | collective-permute-done | bytes 81952 | tf_op jit(solution)/shard_map/ppermute | solution.py:27
  126.5 0.6 collective-permute-done.22
  127.0 2.5 %collective-permute-start.25 = (bf16[2,80,256]{2,1,0:T(8,128)(2,1)S(1)}, bf16[2,80,256]{2,1,0:T(8,128)(2,1)S(1)}, u32[]{:S(2)}, u32[]{:S(2)}) collective-permute-start(bf16[2,80,256]{2,1,0:T(8,128)(2,1)S(1)} %get-tuple-element.57), channel_id=1, source_target_pairs={{0,24},{8,16},{16,8},{24,0},{1,25},{9,17},{17,9},{25,1},{2,26},{10... | collective-permute-start | bytes 245768 | tf_op jit(solution)/shard_map/ppermute | solution.py:27
  129.6 1.6 %collective-permute-start.24 = (bf16[2,80,256]{2,1,0:T(8,128)(2,1)S(1)}, bf16[2,80,256]{2,1,0:T(8,128)(2,1)S(1)}, u32[]{:S(2)}, u32[]{:S(2)}) collective-permute-start(bf16[2,80,256]{2,1,0:T(8,128)(2,1)S(1)} %get-tuple-element.58), channel_id=1, source_target_pairs={{0,8},{8,0},{16,24},{24,16},{1,9},{9,1},{17,25},{25,17},{2,10},{10... | collective-permute-start | bytes 245768 | tf_op jit(solution)/shard_map/ppermute | solution.py:27
  131.2 1.3 collective-permute-done.23
  132.5 0.4 collective-permute-done.25
  132.9 1.1 collective-permute-done.24
  134.1 0.8 pad_maximum_fusion.2
  134.8 4.4 %all-to-all-start.2 = ((f32[8,40,256]{2,1,0:T(8,128)}), f32[8,40,256]{2,1,0:T(8,128)S(1)}, u32[]{:S(2)}, u32[]{:S(2)}) async-start(f32[8,40,256]{2,1,0:T(8,128)} %bitcast.36), calls=%async_computation.2 | async-start | bytes 655360 | tf_op jit(solution)/shard_map/all_to_all | solution.py:208
  139.2 1.8 %fusion.17 = f32[1187,2560]{1,0:T(8,128)S(1)} fusion(bf16[1187,256]{1,0:T(8,128)(2,1)S(1)} %collective-permute-done.26, bf16[2560,256]{1,0:T(8,128)(2,1)S(1)} %collective-permute-done.27), kind=kOutput, calls=%fused_computation.48 | convolution fusion | flops 1555824640 | bytes 14073344 | tf_op jit(solution)/shard_map/dot_general | solution.py:201
  141.0 4.5 %fusion = bf16[1187,2560]{1,0:T(8,128)(2,1)} fusion(f32[1187,2560]{1,0:T(8,128)S(1)} %fusion.17, bf16[1187,256]{1,0:T(8,128)(2,1)S(1)} %get-tuple-element.44, bf16[2560,256]{1,0:T(8,128)(2,1)S(1)} %copy-done.3), kind=kOutput, calls=%fused_computation.1 | convolution fusion | flops 1561902080 | bytes 20150784 | tf_op jit(solution)/shard_map/dot_general | solution.py:201
  145.6 4.8 %all-to-all-done.2 = f32[8,40,256]{2,1,0:T(8,128)S(1)} async-done(((f32[8,40,256]{2,1,0:T(8,128)}), f32[8,40,256]{2,1,0:T(8,128)S(1)}, u32[]{:S(2)}, u32[]{:S(2)}) %all-to-all-start.2) | async-done | bytes 327712 | tf_op jit(solution)/shard_map/all_to_all | solution.py:208
  150.4 0.6 reduce_sum.49
  (36 shorter events, 0.4 us)
Async XLA Ops:
  0.6 53.3 %copy-start = (s32[256]{0:T(256)S(1)}, s32[256]{0:T(256)}, u32[]{:S(2)}) copy-start(s32[256]{0:T(256)} %param.6) | copy-start | bytes 3076
  0.6 32.8 %collective-permute-start.6 = (bf16[1187,2560]{1,0:T(8,128)(2,1)}, bf16[1187,2560]{1,0:T(8,128)(2,1)S(1)}, u32[]{:S(2)}, u32[]{:S(2)}) collective-permute-start(bf16[1187,2560]{1,0:T(8,128)(2,1)} %own_far.3), channel_id=1, source_target_pairs={{0,1},{1,0},{2,3},{3,2},{4,5},{5,4},{6,7},{7,6},{8,9},{9,8},{10,11... | collective-permute-start | bytes 18232328 | tf_op jit(solution)/shard_map/ppermute | solution.py:142
  20.2 5.8 %collective-permute-start.2 = (bf16[2,80,256]{2,1,0:T(8,128)(2,1)S(1)}, bf16[2,80,256]{2,1,0:T(8,128)(2,1)S(1)}, u32[]{:S(2)}, u32[]{:S(2)}) collective-permute-start(bf16[2,80,256]{2,1,0:T(8,128)(2,1)S(1)} %get-tuple-element.63), channel_id=1, source_target_pairs={{0,192},{64,128},{128,64},{192,0},{1,193},{65,129},{129,65},{193,1... | collective-permute-start | bytes 245768 | tf_op jit(solution)/shard_map/ppermute | solution.py:21
  23.0 5.9 %collective-permute-start.1 = (bf16[2,80,256]{2,1,0:T(8,128)(2,1)S(1)}, bf16[2,80,256]{2,1,0:T(8,128)(2,1)S(1)}, u32[]{:S(2)}, u32[]{:S(2)}) collective-permute-start(bf16[2,80,256]{2,1,0:T(8,128)(2,1)S(1)} %get-tuple-element.63), channel_id=1, source_target_pairs={{0,128},{64,192},{128,0},{192,64},{1,129},{65,193},{129,1},{193,65... | collective-permute-start | bytes 245768 | tf_op jit(solution)/shard_map/ppermute | solution.py:21
  23.8 5.8 %collective-permute-start = (bf16[2,80,256]{2,1,0:T(8,128)(2,1)S(1)}, bf16[2,80,256]{2,1,0:T(8,128)(2,1)S(1)}, u32[]{:S(2)}, u32[]{:S(2)}) collective-permute-start(bf16[2,80,256]{2,1,0:T(8,128)(2,1)S(1)} %get-tuple-element.63), channel_id=1, source_target_pairs={{0,64},{64,0},{128,192},{192,128},{1,65},{65,1},{129,193},{193,129... | collective-permute-start | bytes 245768 | tf_op jit(solution)/shard_map/ppermute | solution.py:21
  24.4 5.3 %collective-permute-start.5 = (bf16[2,80,256]{2,1,0:T(8,128)(2,1)S(1)}, bf16[2,80,256]{2,1,0:T(8,128)(2,1)S(1)}, u32[]{:S(2)}, u32[]{:S(2)}) collective-permute-start(bf16[2,80,256]{2,1,0:T(8,128)(2,1)S(1)} %get-tuple-element.64), channel_id=1, source_target_pairs={{0,24},{8,16},{16,8},{24,0},{1,25},{9,17},{17,9},{25,1},{2,26},{10... | collective-permute-start | bytes 245768 | tf_op jit(solution)/shard_map/ppermute | solution.py:21
  26.0 6.0 %collective-permute-start.4 = (bf16[2,80,256]{2,1,0:T(8,128)(2,1)S(1)}, bf16[2,80,256]{2,1,0:T(8,128)(2,1)S(1)}, u32[]{:S(2)}, u32[]{:S(2)}) collective-permute-start(bf16[2,80,256]{2,1,0:T(8,128)(2,1)S(1)} %get-tuple-element.64), channel_id=1, source_target_pairs={{0,16},{8,24},{16,0},{24,8},{1,17},{9,25},{17,1},{25,9},{2,18},{10... | collective-permute-start | bytes 245768 | tf_op jit(solution)/shard_map/ppermute | solution.py:21
  29.0 4.4 %collective-permute-start.3 = (bf16[2,80,256]{2,1,0:T(8,128)(2,1)S(1)}, bf16[2,80,256]{2,1,0:T(8,128)(2,1)S(1)}, u32[]{:S(2)}, u32[]{:S(2)}) collective-permute-start(bf16[2,80,256]{2,1,0:T(8,128)(2,1)S(1)} %get-tuple-element.64), channel_id=1, source_target_pairs={{0,8},{8,0},{16,24},{24,16},{1,9},{9,1},{17,25},{25,17},{2,10},{10... | collective-permute-start | bytes 245768 | tf_op jit(solution)/shard_map/ppermute | solution.py:21
  33.5 13.2 %copy-start.2 = (bf16[1187,2560]{1,0:T(8,128)(2,1)}, bf16[1187,2560]{1,0:T(8,128)(2,1)S(1)}, u32[]{:S(2)}) copy-start(bf16[1187,2560]{1,0:T(8,128)(2,1)S(1)} %collective-permute-done.6.other_far) | copy-start | bytes 18232324
  33.5 13.2 %collective-permute-start.9 = (bf16[4,2,80,256]{3,2,1,0:T(8,128)(2,1)S(1)}, bf16[4,2,80,256]{3,2,1,0:T(8,128)(2,1)S(1)}, u32[]{:S(2)}, u32[]{:S(2)}) collective-permute-start(bf16[4,2,80,256]{3,2,1,0:T(8,128)(2,1)S(1)} %pad_maximum_fusion.a0), channel_id=1, source_target_pairs={{0,24},{8,16},{16,8},{24,0},{1,25},{9,17},{17,9},{25,1},{2,26},{10... | collective-permute-start | bytes 983048 | tf_op jit(solution)/shard_map/ppermute | solution.py:21
  35.2 12.4 %collective-permute-start.8 = (bf16[4,2,80,256]{3,2,1,0:T(8,128)(2,1)S(1)}, bf16[4,2,80,256]{3,2,1,0:T(8,128)(2,1)S(1)}, u32[]{:S(2)}, u32[]{:S(2)}) collective-permute-start(bf16[4,2,80,256]{3,2,1,0:T(8,128)(2,1)S(1)} %pad_maximum_fusion.a0), channel_id=1, source_target_pairs={{0,16},{8,24},{16,0},{24,8},{1,17},{9,25},{17,1},{25,9},{2,18},{10... | collective-permute-start | bytes 983048 | tf_op jit(solution)/shard_map/ppermute | solution.py:21
  36.3 12.4 %collective-permute-start.7 = (bf16[4,2,80,256]{3,2,1,0:T(8,128)(2,1)S(1)}, bf16[4,2,80,256]{3,2,1,0:T(8,128)(2,1)S(1)}, u32[]{:S(2)}, u32[]{:S(2)}) collective-permute-start(bf16[4,2,80,256]{3,2,1,0:T(8,128)(2,1)S(1)} %pad_maximum_fusion.a0), channel_id=1, source_target_pairs={{0,8},{8,0},{16,24},{24,16},{1,9},{9,1},{17,25},{25,17},{2,10},{10... | collective-permute-start | bytes 983048 | tf_op jit(solution)/shard_map/ppermute | solution.py:21
  37.7 13.8 %collective-permute-start.12 = (bf16[4,2,80,256]{3,2,1,0:T(8,128)(2,1)S(1)}, bf16[4,2,80,256]{3,2,1,0:T(8,128)(2,1)S(1)}, u32[]{:S(2)}, u32[]{:S(2)}) collective-permute-start(bf16[4,2,80,256]{3,2,1,0:T(8,128)(2,1)S(1)} %pad_maximum_fusion.1.b0), channel_id=1, source_target_pairs={{0,192},{64,128},{128,64},{192,0},{1,193},{65,129},{129,65},{193,1... | collective-permute-start | bytes 983048 | tf_op jit(solution)/shard_map/ppermute | solution.py:21
  40.8 10.8 %collective-permute-start.11 = (bf16[4,2,80,256]{3,2,1,0:T(8,128)(2,1)S(1)}, bf16[4,2,80,256]{3,2,1,0:T(8,128)(2,1)S(1)}, u32[]{:S(2)}, u32[]{:S(2)}) collective-permute-start(bf16[4,2,80,256]{3,2,1,0:T(8,128)(2,1)S(1)} %pad_maximum_fusion.1.b0), channel_id=1, source_target_pairs={{0,128},{64,192},{128,0},{192,64},{1,129},{65,193},{129,1},{193,65... | collective-permute-start | bytes 983048 | tf_op jit(solution)/shard_map/ppermute | solution.py:21
  46.7 7.2 %collective-permute-start.10 = (bf16[4,2,80,256]{3,2,1,0:T(8,128)(2,1)S(1)}, bf16[4,2,80,256]{3,2,1,0:T(8,128)(2,1)S(1)}, u32[]{:S(2)}, u32[]{:S(2)}) collective-permute-start(bf16[4,2,80,256]{3,2,1,0:T(8,128)(2,1)S(1)} %pad_maximum_fusion.1.b0), channel_id=1, source_target_pairs={{0,64},{64,0},{128,192},{192,128},{1,65},{65,1},{129,193},{193,129... | collective-permute-start | bytes 983048 | tf_op jit(solution)/shard_map/ppermute | solution.py:21
  53.9 39.9 %slice-start = ((s8[6103040]{0:T(1024)(128)(4,1)}), s8[4194304]{0:T(1024)(128)(4,1)S(1)}, s32[]{:S(2)}) async-start(s8[6103040]{0:T(1024)(128)(4,1)} %bitcast.83), calls=%async_computation.3 | async-start | bytes 8388608
  53.9 39.9 %slice-start.1 = ((s8[6103040]{0:T(1024)(128)(4,1)}), s8[1908736]{0:T(1024)(128)(4,1)S(1)}, s32[]{:S(2)}) async-start(s8[6103040]{0:T(1024)(128)(4,1)} %bitcast.83), calls=%async_computation.4 | async-start | bytes 3817472
  65.6 28.1 %copy-start.1 = (f32[256]{0:T(256)S(1)}, f32[256]{0:T(256)}, u32[]{:S(2)}) copy-start(f32[256]{0:T(256)} %param.7) | copy-start | bytes 3076
  86.1 7.6 %collective-permute-start.13 = (f32[3,256]{1,0:T(4,128)S(1)}, f32[3,256]{1,0:T(4,128)S(1)}, u32[]{:S(2)}, u32[]{:S(2)}) collective-permute-start(f32[3,256]{1,0:T(4,128)S(1)} %pad_maximum_fusion.3), channel_id=1, source_target_pairs={{0,32},{32,0},{1,33},{33,1},{2,34},{34,2},{3,35},{35,3},{4,36},{36... | collective-permute-start | bytes 9224 | tf_op jit(solution)/shard_map/ppermute | solution.py:178
  100.5 10.1 %collective-permute-start.14 = (bf16[4,2,80,256]{3,2,1,0:T(8,128)(2,1)S(1)}, bf16[4,2,80,256]{3,2,1,0:T(8,128)(2,1)S(1)}, u32[]{:S(2)}, u32[]{:S(2)}) collective-permute-start(bf16[4,2,80,256]{3,2,1,0:T(8,128)(2,1)S(1)} %get-tuple-element.34), channel_id=1, source_target_pairs={{0,16},{8,24},{16,0},{24,8},{1,17},{9,25},{17,1},{25,9},{2,18},{10... | collective-permute-start | bytes 983048 | tf_op jit(solution)/shard_map/ppermute | solution.py:27
  101.3 11.1 %collective-permute-start.15 = (bf16[4,2,80,256]{3,2,1,0:T(8,128)(2,1)S(1)}, bf16[4,2,80,256]{3,2,1,0:T(8,128)(2,1)S(1)}, u32[]{:S(2)}, u32[]{:S(2)}) collective-permute-start(bf16[4,2,80,256]{3,2,1,0:T(8,128)(2,1)S(1)} %get-tuple-element.35), channel_id=1, source_target_pairs={{0,8},{8,0},{16,24},{24,16},{1,9},{9,1},{17,25},{25,17},{2,10},{10... | collective-permute-start | bytes 983048 | tf_op jit(solution)/shard_map/ppermute | solution.py:27
  102.6 11.4 %collective-permute-start.16 = (bf16[4,2,80,256]{3,2,1,0:T(8,128)(2,1)S(1)}, bf16[4,2,80,256]{3,2,1,0:T(8,128)(2,1)S(1)}, u32[]{:S(2)}, u32[]{:S(2)}) collective-permute-start(bf16[4,2,80,256]{3,2,1,0:T(8,128)(2,1)S(1)} %get-tuple-element.36), channel_id=1, source_target_pairs={{0,24},{8,16},{16,8},{24,0},{1,25},{9,17},{17,9},{25,1},{2,26},{10... | collective-permute-start | bytes 983048 | tf_op jit(solution)/shard_map/ppermute | solution.py:27
  104.7 9.5 %collective-permute-start.17 = (bf16[4,2,80,256]{3,2,1,0:T(8,128)(2,1)S(1)}, bf16[4,2,80,256]{3,2,1,0:T(8,128)(2,1)S(1)}, u32[]{:S(2)}, u32[]{:S(2)}) collective-permute-start(bf16[4,2,80,256]{3,2,1,0:T(8,128)(2,1)S(1)} %get-tuple-element.38), channel_id=1, source_target_pairs={{0,128},{64,192},{128,0},{192,64},{1,129},{65,193},{129,1},{193,65... | collective-permute-start | bytes 983048 | tf_op jit(solution)/shard_map/ppermute | solution.py:27
  105.3 10.1 %collective-permute-start.18 = (bf16[4,2,80,256]{3,2,1,0:T(8,128)(2,1)S(1)}, bf16[4,2,80,256]{3,2,1,0:T(8,128)(2,1)S(1)}, u32[]{:S(2)}, u32[]{:S(2)}) collective-permute-start(bf16[4,2,80,256]{3,2,1,0:T(8,128)(2,1)S(1)} %get-tuple-element.39), channel_id=1, source_target_pairs={{0,64},{64,0},{128,192},{192,128},{1,65},{65,1},{129,193},{193,129... | collective-permute-start | bytes 983048 | tf_op jit(solution)/shard_map/ppermute | solution.py:27
  110.6 9.5 %collective-permute-start.19 = (bf16[4,2,80,256]{3,2,1,0:T(8,128)(2,1)S(1)}, bf16[4,2,80,256]{3,2,1,0:T(8,128)(2,1)S(1)}, u32[]{:S(2)}, u32[]{:S(2)}) collective-permute-start(bf16[4,2,80,256]{3,2,1,0:T(8,128)(2,1)S(1)} %get-tuple-element.40), channel_id=1, source_target_pairs={{0,192},{64,128},{128,64},{192,0},{1,193},{65,129},{129,65},{193,1... | collective-permute-start | bytes 983048 | tf_op jit(solution)/shard_map/ppermute | solution.py:27
  112.4 26.8 %collective-permute-start.27 = (bf16[2560,256]{1,0:T(8,128)(2,1)}, bf16[2560,256]{1,0:T(8,128)(2,1)S(1)}, u32[]{:S(2)}, u32[]{:S(2)}) collective-permute-start(bf16[2560,256]{1,0:T(8,128)(2,1)} %get-tuple-element.46), channel_id=1, source_target_pairs={{0,1},{1,0},{2,3},{3,2},{4,5},{5,4},{6,7},{7,6},{8,9},{9,8},{10,11... | collective-permute-start | bytes 3932168 | tf_op jit(solution)/shard_map/ppermute | solution.py:177
  120.3 6.1 %collective-permute-start.20 = (bf16[2,80,256]{2,1,0:T(8,128)(2,1)S(1)}, bf16[2,80,256]{2,1,0:T(8,128)(2,1)S(1)}, u32[]{:S(2)}, u32[]{:S(2)}) collective-permute-start(bf16[2,80,256]{2,1,0:T(8,128)(2,1)S(1)} %get-tuple-element.53), channel_id=1, source_target_pairs={{0,128},{64,192},{128,0},{192,64},{1,129},{65,193},{129,1},{193,65... | collective-permute-start | bytes 245768 | tf_op jit(solution)/shard_map/ppermute | solution.py:27
  120.4 6.6 %collective-permute-start.22 = (bf16[2,80,256]{2,1,0:T(8,128)(2,1)S(1)}, bf16[2,80,256]{2,1,0:T(8,128)(2,1)S(1)}, u32[]{:S(2)}, u32[]{:S(2)}) collective-permute-start(bf16[2,80,256]{2,1,0:T(8,128)(2,1)S(1)} %get-tuple-element.54), channel_id=1, source_target_pairs={{0,192},{64,128},{128,64},{192,0},{1,193},{65,129},{129,65},{193,1... | collective-permute-start | bytes 245768 | tf_op jit(solution)/shard_map/ppermute | solution.py:27
  121.0 8.5 %collective-permute-start.21 = (bf16[2,80,256]{2,1,0:T(8,128)(2,1)S(1)}, bf16[2,80,256]{2,1,0:T(8,128)(2,1)S(1)}, u32[]{:S(2)}, u32[]{:S(2)}) collective-permute-start(bf16[2,80,256]{2,1,0:T(8,128)(2,1)S(1)} %get-tuple-element.55), channel_id=1, source_target_pairs={{0,64},{64,0},{128,192},{192,128},{1,65},{65,1},{129,193},{193,129... | collective-permute-start | bytes 245768 | tf_op jit(solution)/shard_map/ppermute | solution.py:27
  123.9 15.3 %collective-permute-start.26 = (bf16[1187,256]{1,0:T(8,128)(2,1)S(1)}, bf16[1187,256]{1,0:T(8,128)(2,1)S(1)}, u32[]{:S(2)}, u32[]{:S(2)}) collective-permute-start(bf16[1187,256]{1,0:T(8,128)(2,1)S(1)} %get-tuple-element.44), channel_id=1, source_target_pairs={{0,1},{1,0},{2,3},{3,2},{4,5},{5,4},{6,7},{7,6},{8,9},{9,8},{10,11... | collective-permute-start | bytes 1823240 | tf_op jit(solution)/shard_map/ppermute | solution.py:200
  126.5 6.0 %collective-permute-start.23 = (bf16[2,80,256]{2,1,0:T(8,128)(2,1)S(1)}, bf16[2,80,256]{2,1,0:T(8,128)(2,1)S(1)}, u32[]{:S(2)}, u32[]{:S(2)}) collective-permute-start(bf16[2,80,256]{2,1,0:T(8,128)(2,1)S(1)} %get-tuple-element.56), channel_id=1, source_target_pairs={{0,16},{8,24},{16,0},{24,8},{1,17},{9,25},{17,1},{25,9},{2,18},{10... | collective-permute-start | bytes 245768 | tf_op jit(solution)/shard_map/ppermute | solution.py:27
  127.0 5.8 %collective-permute-start.25 = (bf16[2,80,256]{2,1,0:T(8,128)(2,1)S(1)}, bf16[2,80,256]{2,1,0:T(8,128)(2,1)S(1)}, u32[]{:S(2)}, u32[]{:S(2)}) collective-permute-start(bf16[2,80,256]{2,1,0:T(8,128)(2,1)S(1)} %get-tuple-element.57), channel_id=1, source_target_pairs={{0,24},{8,16},{16,8},{24,0},{1,25},{9,17},{17,9},{25,1},{2,26},{10... | collective-permute-start | bytes 245768 | tf_op jit(solution)/shard_map/ppermute | solution.py:27
  129.6 4.4 %collective-permute-start.24 = (bf16[2,80,256]{2,1,0:T(8,128)(2,1)S(1)}, bf16[2,80,256]{2,1,0:T(8,128)(2,1)S(1)}, u32[]{:S(2)}, u32[]{:S(2)}) collective-permute-start(bf16[2,80,256]{2,1,0:T(8,128)(2,1)S(1)} %get-tuple-element.58), channel_id=1, source_target_pairs={{0,8},{8,0},{16,24},{24,16},{1,9},{9,1},{17,25},{25,17},{2,10},{10... | collective-permute-start | bytes 245768 | tf_op jit(solution)/shard_map/ppermute | solution.py:27
  134.8 15.6 %all-to-all-start.2 = ((f32[8,40,256]{2,1,0:T(8,128)}), f32[8,40,256]{2,1,0:T(8,128)S(1)}, u32[]{:S(2)}, u32[]{:S(2)}) async-start(f32[8,40,256]{2,1,0:T(8,128)} %bitcast.36), calls=%async_computation.2 | async-start | bytes 655360 | tf_op jit(solution)/shard_map/all_to_all | solution.py:208
  139.2 1.8 %copy-start.3 = (bf16[2560,256]{1,0:T(8,128)(2,1)S(1)}, bf16[2560,256]{1,0:T(8,128)(2,1)}, u32[]{:S(2)}) copy-start(bf16[2560,256]{1,0:T(8,128)(2,1)} %get-tuple-element.45) | copy-start | bytes 3932164
